TPU v7x, 32 devices: a whole 2x2x4 slice. The times are simulated.
32 devices in a mesh: member: 2 (over x), region: 16 (over z, y, core).
Axes of the slice: x: 2, y: 2, z: 4, core: 2. Of those that a mesh axis runs over, the one named last changes fastest.
Arguments:
- grid_latent: bfloat16 [32768, 512], P(('member', 'region')), parts along dimension 0, may hold values from -6 to 6
- edge_latent: bfloat16 [98304, 512], P(('member', 'region')), parts along dimension 0, may hold values from -6 to 6
- mesh_latent: bfloat16 [8192, 512], P(('member', 'region')), parts along dimension 0, may hold values from -6 to 6
- sources: int32 [16384, 3], P('region'), may hold values from 0 to 4095, as said below
- w_src: bfloat16 [512, 512], replicated, may hold values from -0.25 to 0.25
- w_edge: bfloat16 [512, 512], replicated, may hold values from -0.25 to 0.25
- w_dst: bfloat16 [512, 512], replicated, may hold values from -0.25 to 0.25
- bias: float32 [512], replicated, may hold values from -3 to 3
- w_out: bfloat16 [512, 84], replicated, may hold values from -0.25 to 0.25
- cotangent: bfloat16 [32768, 84], P(('member', 'region')), parts along dimension 0, may hold values from -6 to 6
Outputs:
- d_grid: bfloat16 [32768, 512], P(('member', 'region')), parts along dimension 0
- d_mesh: float32 [8192, 512], P(('member', 'region')), parts along dimension 0
- d_w_src: float32 [1024, 512], P('member'), parts along dimension 0
- d_w_edge: float32 [1024, 512], P('member'), parts along dimension 0
- d_w_dst: float32 [1024, 512], P('member'), parts along dimension 0
- d_bias: float32 [1024], P('member'), parts along dimension 0
- d_w_out: float32 [1024, 84], P('member'), parts along dimension 0
There are 2 independent parts, one for each index of `member`. A program takes and returns all parts, laid end to end along the dimension named above; an argument that names none is the same for every part. Nothing has to cross between parts.
Inputs may be any that keep to these rules, and one draw needn't show every extreme that they name: `sources`: A grid node g of region r = g // 1024 names only mesh nodes of regions r - 1, r and r + 1 taken cyclically over the regions, where mesh node m lies in region m // 256.
All inputs are finite; a program needn't handle non-finite values.
Results may differ from a plain program's by a relative error of at most 0.012.
Values may be sent and summed in bfloat16 or wider, within the bound.
No kernel may reach another device: no remote copies, remote signals or barrier semaphores. Data moves between devices by JAX's collectives and lax.ppermute only.
A program may use at most 128 MiB of HBM per device.

v0:
```python
import jax
import jax.numpy as jnp
from jax import lax
from jax.sharding import PartitionSpec as P


def padded(block, sides, width):
    for axis, dim in sides:
        count = lax.axis_size(axis)
        forward = [(i, i + 1) for i in range(count - 1)]
        forward.append((count - 1, 0))
        backward = [(target, source) for source, target in forward]
        low = lax.ppermute(
            lax.slice_in_dim(block, block.shape[dim] - width, None, axis=dim), axis, forward
        )
        high = lax.ppermute(lax.slice_in_dim(block, 0, width, axis=dim), axis, backward)
        block = jnp.concatenate([low, block, high], axis=dim)
    return block


def passed_along(block, axis, distance):
    devices = range(lax.axis_size(axis))
    route = [((i - distance) % len(devices), i) for i in devices]
    return lax.ppermute(block, axis, route)


def shards(
    grid_latent, edge_latent, mesh_latent, sources, w_src, w_edge, w_dst, bias, w_out, cotangent
):
    owned = mesh_latent.shape[0]
    nodes = grid_latent.shape[0]
    width = grid_latent.shape[1]
    fan_in = sources.shape[1]
    regions = lax.axis_size("region")
    here = lax.axis_index("region")
    extended = padded(mesh_latent, (("region", 0),), owned)
    local = jnp.mod(sources - (here - 1) * owned, owned * regions).reshape(-1)
    d_agg = jnp.dot(cotangent, w_out.T, preferred_element_type=jnp.float32).astype(jnp.bfloat16)
    src_rows = jnp.take(extended, local, axis=0)
    node_term = jnp.dot(grid_latent, w_dst, preferred_element_type=jnp.float32)
    pre = (
        jnp.dot(src_rows, w_src, preferred_element_type=jnp.float32)
        + jnp.dot(edge_latent, w_edge, preferred_element_type=jnp.float32)
        + jnp.repeat(node_term, fan_in, axis=0)
        + bias
    )
    sig = jax.nn.sigmoid(pre)
    agg = jnp.sum((pre * sig).reshape(nodes, fan_in, width), axis=1).astype(jnp.bfloat16)
    grad_out = jnp.dot(agg.T, cotangent, preferred_element_type=jnp.float32)
    slope = sig * (1.0 + pre * (1.0 - sig))
    d_pre = (jnp.repeat(d_agg.astype(jnp.float32), fan_in, axis=0) * slope).astype(jnp.bfloat16)
    d_node = jnp.sum(d_pre.astype(jnp.float32).reshape(nodes, fan_in, width), axis=1).astype(
        jnp.bfloat16
    )
    mesh_term = jnp.dot(d_pre, w_src.T, preferred_element_type=jnp.float32)
    nearby = jnp.zeros((3 * owned, width), jnp.float32).at[local].add(mesh_term)
    d_mesh = nearby[owned : 2 * owned]
    for offset, block in ((-1, nearby[:owned]), (1, nearby[2 * owned :])):
        d_mesh = d_mesh + passed_along(block.astype(jnp.bfloat16), "region", offset).astype(
            block.dtype
        )
    grad_src = jnp.dot(src_rows.T, d_pre, preferred_element_type=jnp.float32)
    grad_edge = jnp.dot(edge_latent.T, d_pre, preferred_element_type=jnp.float32)
    grad_dst = jnp.dot(grid_latent.T, d_node, preferred_element_type=jnp.float32)
    grad_bias = jnp.sum(d_pre.astype(jnp.float32), axis=0)
    d_grid = jnp.dot(d_node, w_dst.T, preferred_element_type=jnp.float32).astype(jnp.bfloat16)
    total_src, total_edge, total_dst, total_bias, total_out = lax.psum(
        (grad_src, grad_edge, grad_dst, grad_bias, grad_out), "region"
    )
    return (d_grid, d_mesh, total_src, total_edge, total_dst, total_bias, total_out)


def solution(mesh):
    placed = (
        P(("member", "region"), None),
        P(("member", "region"), None),
        P(("member", "region"), None),
        P("region", None),
        P(),
        P(),
        P(),
        P(),
        P(),
        P(("member", "region"), None),
    )
    return jax.shard_map(
        shards,
        mesh=mesh,
        in_specs=placed,
        out_specs=(
            P(("member", "region"), None),
            P(("member", "region"), None),
            P("member", None),
            P("member", None),
            P("member", None),
            P("member"),
            P("member", None),
        ),
        check_vma=False,
    )
```

profile of v0, /device:TPU:0, one launch (start us, length us, event | category | flops | bytes accessed | tf_op | source)
XLA Modules:
  0.0 260.4 jit_solution(893551342392898271)
XLA Ops:
  7.7 5.1 %collective-permute-start.1 = (bf16[256,512]{1,0:T(8,128)(2,1)}, bf16[256,512]{1,0:T(8,128)(2,1)}, u32[]{:S(2)}, u32[]{:S(2)}) collective-permute-start(bf16[256,512]{1,0:T(8,128)(2,1)} %param.12), channel_id=1, source_target_pairs={{1,0},{2,1},{3,2},{4,3},{5,4},{6,5},{7,6},{8,7},{9,8},{10,9},{11,1... | collective-permute-start | bytes 786440 | tf_op jit(solution)/shard_map/ppermute | solution.py:16
  17.3 2.8 %fusion.1 = f32[1024,512]{1,0:T(8,128)} fusion(bf16[1024,84]{0,1:T(8,128)(2,1)} %param.19, bf16[512,84]{0,1:T(8,128)(2,1)} %param.18), kind=kOutput, calls=%fused_computation.9 | convolution fusion | flops 89128960 | bytes 2355200 | tf_op jit(solution)/shard_map/dot_general | solution.py:38
  20.1 3.4 %fusion.15 = f32[1024,512]{1,0:T(8,128)} fusion(bf16[1024,512]{1,0:T(8,128)(2,1)} %param.10, bf16[512,512]{1,0:T(8,128)(2,1)} %param.16), kind=kOutput, calls=%fused_computation.35 | convolution fusion | flops 536870912 | bytes 3670016 | tf_op jit(solution)/shard_map/dot_general | solution.py:40
  23.5 4.5 %fusion.14 = f32[3072,512]{1,0:T(8,128)} fusion(bf16[3072,512]{1,0:T(8,128)(2,1)S(1)} %copy-done, bf16[512,512]{1,0:T(8,128)(2,1)S(1)} %copy-done.4), kind=kOutput, calls=%fused_computation.34 | convolution fusion | flops 1610612736 | bytes 9961472 | tf_op jit(solution)/shard_map/dot_general | solution.py:43
  28.0 6.2 %broadcast_in_dim.24 = f32[1024,3,512]{2,1,0:T(4,128)} broadcast(f32[1024,512]{1,0:T(8,128)} %fusion.15), dimensions={0,2} | broadcast | bytes 8388608 | tf_op jit(solution)/shard_map/broadcast_in_dim | solution.py:44
  34.3 10.7 %reshape.69 = f32[3072,512]{1,0:T(8,128)} reshape(f32[1024,3,512]{2,1,0:T(4,128)} %broadcast_in_dim.24) | data formatting | bytes 12582912 | tf_op jit(solution)/shard_map/reshape | solution.py:44
  45.0 6.2 %broadcast_in_dim.21 = f32[1024,3,512]{2,1,0:T(4,128)} broadcast(f32[1024,512]{1,0:T(8,128)} %fusion.1), dimensions={0,2} | broadcast | bytes 8388608 | tf_op jit(solution)/shard_map/broadcast_in_dim | solution.py:51
  51.2 10.8 %reshape.66 = f32[3072,512]{1,0:T(8,128)} reshape(f32[1024,3,512]{2,1,0:T(4,128)} %broadcast_in_dim.21) | data formatting | bytes 12582912 | tf_op jit(solution)/shard_map/reshape | solution.py:51
  64.0 14.5 %gather_fusion = bf16[3072,512]{1,0:T(8,128)(2,1)} fusion(bf16[768,512]{1,0:T(8,128)(2,1)} %pad_maximum_fusion, s32[3072]{0:T(1024)S(1)} %broadcast_clamp_fusion), kind=kCustom, calls=%fused_computation | custom fusion | bytes 6303744 | tf_op jit(solution)/shard_map/jit(_take)/gather | solution.py:39
  78.6 12.1 %convert_reduce_fusion = (f32[512]{0:T(512)S(1)}, bf16[3072,512]{1,0:T(8,128)(2,1)S(1)}, f32[3072,512]{1,0:T(8,128)}) fusion(f32[3072,512]{1,0:T(8,128)} %reshape.66, f32[512]{0:T(512)S(1)} %copy-done.7, f32[3072,512]{1,0:T(8,128)} %reshape.69, f32[3072,512]{1,0:T(8,128)} %fusion.14, bf16[512,512]{1,0:T(8,128)(2,1)} %param.14, ...), kind=kOutput, calls=%fused_computation.7 | convolution fusion | flops 1635778048 | bytes 31988736 | tf_op jit(solution)/shard_map/dot_general | solution.py:42
  90.7 2.9 %fusion.2 = f32[512,512]{1,0:T(8,128)} fusion(bf16[3072,512]{1,0:T(8,128)(2,1)S(1)} %get-tuple-element.26, bf16[3072,512]{1,0:T(8,128)(2,1)S(1)} %copy-done.2, pred[3072]{0:T(1024)(128)(4,1)S(1)} %compare_and_fusion), kind=kOutput, calls=%fused_computation.13 | convolution fusion | flops 1612185600 | bytes 7343104 | tf_op jit(solution)/shard_map/dot_general | solution.py:62
  93.6 2.8 %convolution_bitcast_fusion.1 = f32[512,512]{0,1:T(8,128)} fusion(bf16[3072,512]{1,0:T(8,128)(2,1)S(1)} %get-tuple-element.26, bf16[3072,512]{1,0:T(8,128)(2,1)S(1)} %copy-done), kind=kOutput, calls=%fused_computation.12 | convolution fusion | flops 1610612736 | bytes 7340032 | tf_op jit(solution)/shard_map/dot_general | solution.py:63
  96.4 9.7 %reshape.70 = f32[1024,3,512]{2,1,0:T(4,128)} reshape(bf16[3072,512]{1,0:T(8,128)(2,1)} %copy-done.1) | data formatting | bytes 9437184 | tf_op jit(solution)/shard_map/reshape | solution.py:52
  106.1 9.4 %reduce_sum.27 = bf16[1024,512]{1,0:T(8,128)(2,1)} reduce(f32[1024,3,512]{2,1,0:T(4,128)} %reshape.70, f32[]{:T(128)} %constant.45.clone.1), dimensions={1}, to_apply=%region_0.1 | reduce | flops 1048576 | bytes 7340036 | tf_op jit(solution)/shard_map/reduce_sum | solution.py:52
  115.5 3.2 %convolution_bitcast_fusion = f32[512,512]{0,1:T(8,128)} fusion(bf16[1024,512]{1,0:T(8,128)(2,1)} %param.10, bf16[1024,512]{1,0:T(8,128)(2,1)} %reduce_sum.27), kind=kOutput, calls=%fused_computation.11 | convolution fusion | flops 536870912 | bytes 3145728 | tf_op jit(solution)/shard_map/dot_general | solution.py:64
  118.8 10.5 %reshape.71 = f32[1024,3,512]{2,1,0:T(4,128)} reshape(f32[3072,512]{1,0:T(8,128)} %get-tuple-element.27) | data formatting | bytes 12582912 | tf_op jit(solution)/shard_map/reshape | solution.py:48
  129.3 9.4 %reduce_sum.29 = bf16[1024,512]{1,0:T(8,128)(2,1)} reduce(f32[1024,3,512]{2,1,0:T(4,128)} %reshape.71, f32[]{:T(128)} %constant.45.clone.1), dimensions={1}, to_apply=%region_7.8 | reduce | flops 1048576 | bytes 7340036 | tf_op jit(solution)/shard_map/reduce_sum | solution.py:48
  141.0 6.5 %fusion.16 = f32[3072,512]{1,0:T(8,128)} fusion(bf16[3072,512]{1,0:T(8,128)(2,1)} %copy-done.1, bf16[512,512]{1,0:T(8,128)(2,1)} %param.14), kind=kOutput, calls=%fused_computation.36 | convolution fusion | flops 1610612736 | bytes 9961472 | tf_op jit(solution)/shard_map/dot_general | solution.py:55
  147.4 20.4 %scatter_custom_fusion = f32[768,512]{1,0:T(8,128)} fusion(s32[3072]{0:T(1024)S(1)} %bitcast.24, f32[3072,512]{1,0:T(8,128)} %fusion.16, f32[]{:T(128)} %constant.45.clone.1), kind=kCustom, calls=%fused_computation.17 | custom fusion | flops 1572864 | bytes 1573376 | tf_op jit(solution)/shard_map/scatter-add | solution.py:56
  171.0 34.5 %psum.38 = f32[512]{0:T(512)} all-reduce(f32[512]{0:T(512)S(1)} %get-tuple-element.25), channel_id=1, replica_groups=mesh['member'=2,'region'=16] {'region'}, use_global_device_ids=true, to_apply=%region_6.7 | all-reduce | flops 512 | bytes 4096 | tf_op jit(solution)/shard_map/psum | solution.py:67
  205.5 3.1 %convolution_convert_fusion.1 = bf16[1024,512]{1,0:T(8,128)(2,1)} fusion(bf16[512,512]{1,0:T(8,128)(2,1)} %param.16, bf16[1024,512]{1,0:T(8,128)(2,1)} %reduce_sum.27), kind=kOutput, calls=%fused_computation.10 | convolution fusion | flops 537395200 | bytes 2621440 | tf_op jit(solution)/shard_map/dot_general | solution.py:66
  210.6 34.9 %all-reduce.3.cloned.1.call-done = (f32[512,512]{1,0:T(8,128)}, f32[512,512]{0,1:T(8,128)}, f32[512,512]{0,1:T(8,128)}, f32[512,84]{0,1:T(8,128)}) async-done(((f32[512,512]{1,0:T(8,128)}, f32[512,512]{0,1:T(8,128)}, f32[512,512]{0,1:T(8,128)}, f32[512,84]{0,1:T(8,128)}), (f32[512,512]{1,0:T(8,128)}, f32[512,512]{0,1:T(8,128)}, f32[512,512]{0,1:T(8,128)}, f32[512,84]{0,1:T(8,128)})) %all-reduce.3.cloned.1.call-update) | async-done | bytes 3317776 | tf_op jit(solution)/shard_map/psum | solution.py:67
  245.5 2.6 copy.21
  248.1 2.5 copy.22
  (39 shorter events, 17.4 us)
Async XLA Ops:
  7.2 16.3 %copy-start = (bf16[3072,512]{1,0:T(8,128)(2,1)S(1)}, bf16[3072,512]{1,0:T(8,128)(2,1)}, u32[]{:S(2)}) copy-start(bf16[3072,512]{1,0:T(8,128)(2,1)} %param.11) | copy-start | bytes 9437188
  7.2 238.3 %all-reduce.3.cloned.1.call-start = ((), (), s32[]{:S(2)}) async-start(), calls=%async_computation | async-start | bytes 6651904 | tf_op jit(solution)/shard_map/psum | solution.py:67
  7.2 54.8 %collective-permute-start = (bf16[256,512]{1,0:T(8,128)(2,1)}, bf16[256,512]{1,0:T(8,128)(2,1)}, u32[]{:S(2)}, u32[]{:S(2)}) collective-permute-start(bf16[256,512]{1,0:T(8,128)(2,1)} %param.12), channel_id=1, source_target_pairs={{0,1},{1,2},{2,3},{3,4},{4,5},{5,6},{6,7},{7,8},{8,9},{9,10},{10,1... | collective-permute-start | bytes 786440 | tf_op jit(solution)/shard_map/ppermute | solution.py:13
  7.7 54.3 %collective-permute-start.1 = (bf16[256,512]{1,0:T(8,128)(2,1)}, bf16[256,512]{1,0:T(8,128)(2,1)}, u32[]{:S(2)}, u32[]{:S(2)}) collective-permute-start(bf16[256,512]{1,0:T(8,128)(2,1)} %param.12), channel_id=1, source_target_pairs={{1,0},{2,1},{3,2},{4,3},{5,4},{6,5},{7,6},{8,7},{9,8},{10,9},{11,1... | collective-permute-start | bytes 786440 | tf_op jit(solution)/shard_map/ppermute | solution.py:16
  17.3 6.2 %copy-start.4 = (bf16[512,512]{1,0:T(8,128)(2,1)S(1)}, bf16[512,512]{1,0:T(8,128)(2,1)}, u32[]{:S(2)}) copy-start(bf16[512,512]{1,0:T(8,128)(2,1)} %param.15) | copy-start | bytes 1572868
  51.2 10.8 %copy-start.5 = (bf16[256,512]{1,0:T(8,128)(2,1)S(1)}, bf16[256,512]{1,0:T(8,128)(2,1)}, u32[]{:S(2)}) copy-start(bf16[256,512]{1,0:T(8,128)(2,1)} %param.12) | copy-start | bytes 786436
  64.0 14.5 %copy-start.7 = (f32[512]{0:T(512)S(1)}, f32[512]{0:T(512)}, u32[]{:S(2)}) copy-start(f32[512]{0:T(512)} %param.17) | copy-start | bytes 6148
  78.6 12.1 %copy-start.2 = (bf16[3072,512]{1,0:T(8,128)(2,1)S(1)}, bf16[3072,512]{1,0:T(8,128)(2,1)}, u32[]{:S(2)}) copy-start(bf16[3072,512]{1,0:T(8,128)(2,1)} %gather_fusion) | copy-start | bytes 9437188
  90.7 2.9 %copy-start.1 = (bf16[3072,512]{1,0:T(8,128)(2,1)}, bf16[3072,512]{1,0:T(8,128)(2,1)S(1)}, u32[]{:S(2)}) copy-start(bf16[3072,512]{1,0:T(8,128)(2,1)S(1)} %get-tuple-element.26) | copy-start | bytes 9437188
  129.3 9.4 %copy-start.3 = (bf16[1024,84]{0,1:T(8,128)(2,1)S(1)}, bf16[1024,84]{0,1:T(8,128)(2,1)}, u32[]{:S(2)}) copy-start(bf16[1024,84]{0,1:T(8,128)(2,1)} %param.19) | copy-start | bytes 516100
  170.2 38.4 %collective-permute-start.2 = (bf16[256,512]{1,0:T(8,128)(2,1)}, bf16[256,512]{1,0:T(8,128)(2,1)S(1)}, u32[]{:S(2)}, u32[]{:S(2)}) collective-permute-start(bf16[256,512]{1,0:T(8,128)(2,1)} %get-tuple-element.28), channel_id=1, source_target_pairs={{1,0},{2,1},{3,2},{4,3},{5,4},{6,5},{7,6},{8,7},{9,8},{10,9},{11,1... | collective-permute-start | bytes 786440 | tf_op jit(solution)/shard_map/ppermute | solution.py:24
  171.0 37.6 %collective-permute-start.3 = (bf16[256,512]{1,0:T(8,128)(2,1)}, bf16[256,512]{1,0:T(8,128)(2,1)}, u32[]{:S(2)}, u32[]{:S(2)}) collective-permute-start(bf16[256,512]{1,0:T(8,128)(2,1)} %get-tuple-element.29), channel_id=1, source_target_pairs={{15,0},{0,1},{1,2},{2,3},{3,4},{4,5},{5,6},{6,7},{7,8},{8,9},{9,10... | collective-permute-start | bytes 786440 | tf_op jit(solution)/shard_map/ppermute | solution.py:24
  245.5 7.4 %copy-start.6 = (f32[512,84]{0,1:T(8,128)S(1)}, f32[512,84]{0,1:T(8,128)}, u32[]{:S(2)}) copy-start(f32[512,84]{0,1:T(8,128)} %get-tuple-element.36) | copy-start | bytes 516100
Sparse Core Ops, SparseCore 0:
  141.1 104.3 all-reduce.2
where the time goes:
time: 262 us; the launch traced here: 260 us
  local copies, waits for them, and re-layouts  81.4 us (31%)
  other arithmetic  45.5 us (17%)
  matrix products  43.5 us (17%)
  waiting for transfers between devices  34.9 us (13%)
  blocking collectives  34.5 us (13%)
  between operations  14.1 us (5%)
  starting transfers between devices  6.37 us (2%)
    psum x1, waiting for transfers between devices, shards(): lax.psum((grad_src, grad_edge, grad_dst, grad_bias, grad_out), 'region')  34.9 us
    psum x1, blocking collectives, shards(): lax.psum((grad_src, grad_edge, grad_dst, grad_bias, grad_out), 'region')  34.5 us
    scatter-add x1, other arithmetic, shards(): nearby = jnp.zeros((3 * owned, width), jnp.float32).at[local].add(mesh_term)  20.4 us
    gather x1, local copies, waits for them, and re-layouts, shards(): src_rows = jnp.take(extended, local, axis=0)  14.5 us
    dot_general x1, matrix products, shards(): jnp.dot(src_rows, w_src, preferred_element_type=jnp.float32)  12.1 us
    reshape x1, local copies, waits for them, and re-layouts, shards(): jnp.repeat(d_agg.astype(jnp.float32), fan_in, axis=0) * slope  10.8 us
    reshape x1, local copies, waits for them, and re-layouts, shards(): jnp.repeat(node_term, fan_in, axis=0)  10.7 us
    reshape x1, local copies, waits for them, and re-layouts, shards(): (pre * sig).reshape(nodes, fan_in, width)  10.5 us
  transfers between devices with their start and end apart: 5, of which 1 were waited for; matrix products, arithmetic and copies ran while one was open for 32% of the time, Pallas kernels for 0%

commit v1 on v0

v1 whole, which is shorter than its diff:
```python
import functools

import jax
import jax.numpy as jnp
from jax import lax
from jax.experimental import pallas as pl
from jax.experimental.pallas import tpu as pltpu
from jax.sharding import PartitionSpec as P

BF16 = jnp.bfloat16
F32 = jnp.float32
TILE = 256
NT = (((1,), (1,)), ((), ()))
TN = (((0,), (0,)), ((), ()))
VMEM_LIMIT = 40 * 1024 * 1024


def dot(a, b, dims=(((1,), (0,)), ((), ()))):
    return lax.dot_general(a, b, dims, preferred_element_type=F32)


def params():
    return pltpu.CompilerParams(vmem_limit_bytes=VMEM_LIMIT)


def base_kernel(fan, edge, grid, cot, w_edge, w_dst, w_out, bias, planes, base, d_agg, wide):
    lanes = wide.shape[2]
    for c in range(wide.shape[0]):
        wide[c] = edge[:, c * lanes : (c + 1) * lanes].astype(F32)
    node = dot(grid[...], w_dst[...]) + bias[...]
    rows = grid.shape[0]
    for k in range(fan):
        pieces = [wide[c, pl.ds(k, rows, stride=fan), :] for c in range(wide.shape[0])]
        plane = jnp.concatenate(pieces, axis=1).astype(BF16)
        planes[k] = plane
        base[k] = node
        base[k] += dot(plane, w_edge[...])
    d_agg[...] = dot(cot[...], w_out[...], NT).astype(BF16)


def base_call(edge, grid, cot, w_edge, w_dst, w_out, bias):
    nodes, width = grid.shape
    fan = edge.shape[0] // nodes
    outs = cot.shape[1]
    whole = lambda *shape: pl.BlockSpec(shape, lambda i: (0,) * len(shape))
    return pl.pallas_call(
        functools.partial(base_kernel, fan),
        grid=(nodes // TILE,),
        in_specs=[
            pl.BlockSpec((fan * TILE, width), lambda i: (i, 0)),
            pl.BlockSpec((TILE, width), lambda i: (i, 0)),
            pl.BlockSpec((TILE, outs), lambda i: (i, 0)),
            whole(width, width),
            whole(width, width),
            whole(width, outs),
            whole(1, width),
        ],
        out_specs=[
            pl.BlockSpec((fan, TILE, width), lambda i: (0, i, 0)),
            pl.BlockSpec((fan, TILE, width), lambda i: (0, i, 0)),
            pl.BlockSpec((TILE, width), lambda i: (i, 0)),
        ],
        out_shape=[
            jax.ShapeDtypeStruct((fan, nodes, width), BF16),
            jax.ShapeDtypeStruct((fan, nodes, width), F32),
            jax.ShapeDtypeStruct((nodes, width), BF16),
        ],
        scratch_shapes=[pltpu.VMEM((width // 128, fan * TILE, 128), F32)],
        compiler_params=params(),
        name="base_terms",
    )(edge, grid, cot, w_edge, w_dst, w_out, bias)


def column_kernel(
    fan, base, planes, d_agg, grid, cot, src, src_t, low, own, high, w_src,
    packed, d_node, sums, proj, acc, g_edge, g_dst, g_out, g_bias,
):
    step = pl.program_id(0)
    width = grid.shape[1]
    owned = own.shape[0]
    outs = cot.shape[1]

    @pl.when(step == 0)
    def _():
        for j, part in enumerate((low, own, high)):
            proj[j * owned : (j + 1) * owned] = dot(part[...], w_src[...]).astype(BF16)
        for total in (acc, g_edge, g_dst, g_out, g_bias):
            total[...] = jnp.zeros_like(total)

    rows = grid.shape[0]
    near = 3 * owned
    upstream = d_agg[...].astype(F32)
    silu_sum = jnp.zeros(upstream.shape, F32)
    node_sum = jnp.zeros(upstream.shape, F32)
    for k in range(fan):
        hit = lax.broadcasted_iota(jnp.int32, (rows, near), 1) == src[:, k : k + 1]
        pick = jnp.where(hit, 1.0, 0.0).astype(BF16)
        pre = base[k] + dot(pick, proj[...])
        sig = 0.5 + 0.5 * jnp.tanh(0.5 * pre)
        silu = pre * sig
        silu_sum += silu
        d_pre = (upstream * (sig + silu * (1.0 - sig))).astype(BF16)
        node_sum += d_pre.astype(F32)
        hit_t = lax.broadcasted_iota(jnp.int32, (near, rows), 0) == src_t[k : k + 1, :]
        pick_t = jnp.where(hit_t, 1.0, 0.0).astype(BF16)
        acc[...] += dot(pick_t, d_pre)
        g_edge[...] += dot(planes[k], d_pre, TN)
    agg = silu_sum.astype(BF16)
    node = node_sum.astype(BF16)
    d_node[...] = node
    g_out[...] += dot(cot[...], agg, TN)
    g_dst[...] += dot(grid[...], node, TN)
    g_bias[...] += jnp.sum(node_sum.reshape(rows // 8, 8, node_sum.shape[1]), axis=0)

    @pl.when(step == pl.num_programs(0) - 1)
    def _():
        total = acc[...].astype(BF16)
        sums[...] = total
        g_src = jnp.zeros(g_edge.shape, F32)
        for j, part in enumerate((low, own, high)):
            g_src += dot(part[...], total[j * owned : (j + 1) * owned], TN)
        packed[0:width] = g_src.astype(BF16)
        packed[width : 2 * width] = g_edge[...].astype(BF16)
        packed[2 * width : 3 * width] = g_dst[...].astype(BF16)
        tail = packed.shape[0] - 3 * width
        bias_row = jnp.sum(g_bias[...], axis=0, keepdims=True)
        place = lax.broadcasted_iota(jnp.int32, (tail, bias_row.shape[1]), 0)
        out_rows = jnp.concatenate(
            [g_out[...], jnp.zeros((tail - g_out.shape[0], bias_row.shape[1]), F32)], axis=0
        )
        packed[3 * width :] = jnp.where(place == outs, bias_row, out_rows).astype(BF16)


def column_call(h, parts, base, planes, d_agg, grid, cot, src, src_t, low, own, high, w_src, rows):
    fan, nodes, width = planes.shape
    cols = width // parts
    outs = cot.shape[1]
    owned = own.shape[0]
    near = 3 * owned
    whole = lambda *shape: pl.BlockSpec(shape, lambda i: (0,) * len(shape))
    return pl.pallas_call(
        functools.partial(column_kernel, fan),
        grid=(nodes // TILE,),
        in_specs=[
            pl.BlockSpec((fan, TILE, cols), lambda i: (0, i, h)),
            pl.BlockSpec((fan, TILE, width), lambda i: (0, i, 0)),
            pl.BlockSpec((TILE, cols), lambda i: (i, h)),
            pl.BlockSpec((TILE, width), lambda i: (i, 0)),
            pl.BlockSpec((TILE, outs), lambda i: (i, 0)),
            pl.BlockSpec((TILE, fan), lambda i: (i, 0)),
            pl.BlockSpec((fan, TILE), lambda i: (0, i)),
            whole(owned, width),
            whole(owned, width),
            whole(owned, width),
            pl.BlockSpec((width, cols), lambda i: (0, h)),
        ],
        out_specs=[
            whole(rows, cols),
            pl.BlockSpec((TILE, cols), lambda i: (i, 0)),
            whole(near, cols),
        ],
        out_shape=[
            jax.ShapeDtypeStruct((rows, cols), BF16),
            jax.ShapeDtypeStruct((nodes, cols), BF16),
            jax.ShapeDtypeStruct((near, cols), BF16),
        ],
        scratch_shapes=[
            pltpu.VMEM((near, cols), BF16),
            pltpu.VMEM((near, cols), F32),
            pltpu.VMEM((width, cols), F32),
            pltpu.VMEM((width, cols), F32),
            pltpu.VMEM((outs, cols), F32),
            pltpu.VMEM((8, cols), F32),
        ],
        compiler_params=params(),
        name=f"columns_{h}",
    )(base, planes, d_agg, grid, cot, src, src_t, low, own, high, w_src)


def exchanged(block, partner_of):
    regions = lax.axis_size("region")
    return lax.ppermute(block, "region", [(i, partner_of(i)) for i in range(regions)])


def orders(regions):
    bits = [1 << b for b in range(1, regions.bit_length() - 1)]
    other = list(bits)
    if len(other) > 1:
        other[0], other[1] = other[1], other[0]
    return [1] + bits, [1] + other


def total_over_regions(block):
    regions = lax.axis_size("region")
    here = lax.axis_index("region")
    even, odd = orders(regions)
    stages = []
    for a, b in zip(even, odd):
        side = jnp.where(here % 2 == 0, (here // a) % 2, (here // b) % 2)
        stages.append((side, lambda i, a=a, b=b: i ^ (b if i % 2 else a)))
    for side, partner in stages:
        half = block.shape[0] // 2
        send = lax.dynamic_slice_in_dim(block, (1 - side) * half, half, 0).astype(BF16)
        arrived = exchanged(send, partner)
        keep = lax.dynamic_slice_in_dim(block, side * half, half, 0)
        block = keep.astype(F32) + arrived.astype(F32)
    block = block.astype(BF16)
    for side, partner in reversed(stages):
        arrived = exchanged(block, partner)
        block = jnp.where(
            side == 0, jnp.concatenate([block, arrived]), jnp.concatenate([arrived, block])
        )
    return block


def ring(regions, distance):
    return lambda i: (i + distance) % regions


def shards(
    grid_latent, edge_latent, mesh_latent, sources, w_src, w_edge, w_dst, bias, w_out, cotangent
):
    owned, width = mesh_latent.shape
    outs = cotangent.shape[1]
    regions = lax.axis_size("region")
    here = lax.axis_index("region")
    low = exchanged(mesh_latent, ring(regions, 1))
    high = exchanged(mesh_latent, ring(regions, -1))
    local = jnp.mod(sources - (here - 1) * owned, owned * regions)
    base, planes, d_agg = None, None, None
    planes, base, d_agg = base_call(
        edge_latent, grid_latent, cotangent, w_edge, w_dst, w_out, bias.reshape(1, -1)
    )
    unit = 8 * regions
    rows = -(-(3 * width + outs + 1) // unit) * unit
    parts = 2
    packed, d_node, sums = [], [], []
    for h in range(parts):
        a, b, c = column_call(
            h, parts, base, planes, d_agg, grid_latent, cotangent, local, local.T,
            low, mesh_latent, high, w_src, rows,
        )
        packed.append(a)
        d_node.append(b)
        sums.append(c)
    totals = [total_over_regions(block) for block in packed]
    sums = jnp.concatenate(sums, axis=1)
    d_mesh_in = (
        sums[owned : 2 * owned].astype(F32)
        + exchanged(sums[:owned], ring(regions, -1)).astype(F32)
        + exchanged(sums[2 * owned :], ring(regions, 1)).astype(F32)
    ).astype(BF16)
    d_mesh = dot(d_mesh_in, w_src, NT)
    d_grid = dot(jnp.concatenate(d_node, axis=1), w_dst, NT).astype(BF16)
    total = jnp.concatenate(totals, axis=1).astype(F32)
    return (
        d_grid,
        d_mesh,
        total[:width],
        total[width : 2 * width],
        total[2 * width : 3 * width],
        total[3 * width + outs],
        total[3 * width : 3 * width + outs].T,
    )


def solution(mesh):
    placed = (
        P(("member", "region"), None),
        P(("member", "region"), None),
        P(("member", "region"), None),
        P("region", None),
        P(),
        P(),
        P(),
        P(),
        P(),
        P(("member", "region"), None),
    )
    return jax.shard_map(
        shards,
        mesh=mesh,
        in_specs=placed,
        out_specs=(
            P(("member", "region"), None),
            P(("member", "region"), None),
            P("member", None),
            P("member", None),
            P("member", None),
            P("member"),
            P("member", None),
        ),
        check_vma=False,
    )
```

time: 262 us -> 101 us (0.39)
  local copies, waits for them, and re-layouts: 81.4 us -> 19.6 us
  other arithmetic: 45.5 us -> 4.74 us
  matrix products: 43.5 us -> 2.85 us
  blocking collectives: 34.5 us -> 0 us
  Pallas kernels: 0 us -> 25.6 us
  between operations: 14.1 us -> 1.03 us
  starting transfers between devices: 6.37 us -> 19.2 us
  waiting for transfers between devices: 34.9 us -> 27.7 us
    reshape x6 -> x0, local copies, waits for them, and re-layouts: 44.5 us -> none  [the longest x1 10.8 us: shards(): jnp.repeat(d_agg.astype(jnp.float32), fan_in, axis=0) * slope]
    dot_general x10 -> x2, matrix products: 43.5 us -> 2.85 us  [dot(): return lax.dot_general(a, b, dims, preferred_element_type=F32)]
    psum x1 -> x0, waiting for transfers between devices: 34.9 us -> none  [shards(): lax.psum((grad_src, grad_edge, grad_dst, grad_bias, grad_out), 'region')]
    psum x1 -> x0, blocking collectives: 34.5 us -> none  [shards(): lax.psum((grad_src, grad_edge, grad_dst, grad_bias, grad_out), 'region')]
    ppermute x4 -> x20, waiting for transfers between devices: 0.01 us -> 27.7 us  [exchanged(): lax.ppermute(block, 'region', [(i, partner_of(i)) for i in range(regions)])]
    pallas_call x0 -> x3, Pallas kernels: none -> 25.6 us  [the longest x2 20.6 us: column_call(): pl.pallas_call(functools.partial(column_kernel, fan), grid=(nodes // TILE...]
    scatter-add x1 -> x0, other arithmetic: 20.4 us -> none  [shards(): nearby = jnp.zeros((3 * owned, width), jnp.float32).at[local].add(mesh_term)]
    reduce_sum x2 -> x0, other arithmetic: 18.9 us -> none  [the longest x1 9.44 us: shards(): jnp.sum((pre * sig).reshape(nodes, fan_in, width), axis=1)]
  transfers between devices with their start and end apart: 5 -> 20, of which waited for: 1 -> 12; matrix products, arithmetic and copies ran while one was open for 32% -> 9% of each run, Pallas kernels for 0% -> 15%
where the time goes in v1:
time: 101 us
  waiting for transfers between devices  27.7 us (27%)
  Pallas kernels  25.6 us (25%)
  local copies, waits for them, and re-layouts  19.6 us (19%)
  starting transfers between devices  19.2 us (19%)
  other arithmetic  4.74 us (5%)
  matrix products  2.85 us (3%)
  between operations  1.03 us (1%)
    ppermute x20, waiting for transfers between devices, exchanged(): lax.ppermute(block, 'region', [(i, partner_of(i)) for i in range(regions)])  27.7 us
    pallas_call x2, Pallas kernels, column_call(): pl.pallas_call(functools.partial(column_kernel, fan), grid=(nodes // TILE...  20.6 us
    ppermute x20, starting transfers between devices, exchanged(): lax.ppermute(block, 'region', [(i, partner_of(i)) for i in range(regions)])  19.2 us
    unnamed x47, local copies, waits for them, and re-layouts  15.8 us
    pallas_call x1, Pallas kernels, base_call(): pl.pallas_call(functools.partial(base_kernel, fan), grid=(nodes // TILE,)...  5.07 us
    dot_general x2, matrix products, dot(): return lax.dot_general(a, b, dims, preferred_element_type=F32)  2.85 us
  transfers between devices with their start and end apart: 20, of which 12 were waited for; matrix products, arithmetic and copies ran while one was open for 9% of the time, Pallas kernels for 15%

profile of v1, /device:TPU:0, one launch (start us, length us, event | category | flops | bytes accessed | tf_op | source)
XLA Modules:
  0.0 100.7 jit_solution(8539861246856362063)
XLA Ops:
  1.1 5.1 %collective-permute-start.1 = (bf16[256,512]{1,0:T(8,128)(2,1)}, bf16[256,512]{1,0:T(8,128)(2,1)}, u32[]{:S(2)}, u32[]{:S(2)}) collective-permute-start(bf16[256,512]{1,0:T(8,128)(2,1)} %own.3), channel_id=1, source_target_pairs={{0,15},{1,0},{2,1},{3,2},{4,3},{5,4},{6,5},{7,6},{8,7},{9,8},{10,9... | collective-permute-start | bytes 786440 | tf_op jit(solution)/shard_map/ppermute | solution.py:182
  10.1 1.2 %copy-done = bf16[1024,512]{1,0:T(8,128)(2,1)S(1)} copy-done((bf16[1024,512]{1,0:T(8,128)(2,1)S(1)}, bf16[1024,512]{1,0:T(8,128)(2,1)}, u32[]{:S(2)}) %copy-start) | copy-done | bytes 1048600
  11.3 1.9 %copy-done.8 = bf16[3072,512]{1,0:T(8,128)(2,1)S(1)} copy-done((bf16[3072,512]{1,0:T(8,128)(2,1)S(1)}, bf16[3072,512]{1,0:T(8,128)(2,1)}, u32[]{:S(2)}) %copy-start.8) | copy-done | bytes 3145752
  16.0 5.1 %base_terms.1 = (bf16[3,1024,512]{2,1,0:T(8,128)(2,1)S(1)}, f32[3,1024,512]{2,1,0:T(8,128)}, bf16[1024,512]{1,0:T(8,128)(2,1)S(1)}) custom-call(bf16[3072,512]{1,0:T(8,128)(2,1)S(1)} %copy-done.8, bf16[1024,512]{1,0:T(8,128)(2,1)S(1)} %copy-done, bf16[1024,84]{1,0:T(8,128)(2,1)S(1)} %copy.17.cot, bf16[512,512]{1,0:T(8,128)(2,1)S(1)} %copy-done.13, ...), custom_call_target="tpu_custom_call" | custom-call | tf_op jit(solution)/shard_map/base_terms/pallas_call | solution.py:46
  21.1 10.4 %columns_1.1 = (bf16[1664,256]{1,0:T(8,128)(2,1)S(1)}, bf16[1024,256]{1,0:T(8,128)(2,1)S(1)}, bf16[768,256]{1,0:T(8,128)(2,1)S(1)}) custom-call(f32[3,1024,512]{2,1,0:T(8,128)} %get-tuple-element.16.base, bf16[3,1024,512]{2,1,0:T(8,128)(2,1)S(1)} %get-tuple-element.17.planes, bf16[1024,512]{1,0:T(8,128)(2,1)S(1)} %get-tuple-element.18.d_agg, ...), custom_call_target="tpu_custom_call" | custom-call | tf_op jit(solution)/shard_map/columns_1/pallas_call | solution.py:141
  34.1 1.2 %copy-done.1 = bf16[1024,512]{1,0:T(8,128)(2,1)S(1)} copy-done((bf16[1024,512]{1,0:T(8,128)(2,1)S(1)}, bf16[1024,512]{1,0:T(8,128)(2,1)}, u32[]{:S(2)}) %copy-start.1) | copy-done | bytes 1048600
  37.4 1.2 %copy-done.7 = bf16[1024,512]{1,0:T(8,128)(2,1)S(1)} copy-done((bf16[1024,512]{1,0:T(8,128)(2,1)S(1)}, bf16[1024,512]{1,0:T(8,128)(2,1)}, u32[]{:S(2)}) %copy-start.7) | copy-done | bytes 1048600
  39.6 10.1 %columns_0.1 = (bf16[1664,256]{1,0:T(8,128)(2,1)S(1)}, bf16[1024,256]{1,0:T(8,128)(2,1)S(1)}, bf16[768,256]{1,0:T(8,128)(2,1)S(1)}) custom-call(f32[3,1024,512]{2,1,0:T(8,128)} %get-tuple-element.16.base, bf16[3,1024,512]{2,1,0:T(8,128)(2,1)S(1)} %get-tuple-element.17.planes, bf16[1024,512]{1,0:T(8,128)(2,1)S(1)} %copy-done.7, ...), custom_call_target="tpu_custom_call" | custom-call | tf_op jit(solution)/shard_map/columns_0/pallas_call | solution.py:141
  52.4 2.1 %collective-permute-start.5 = (bf16[416,256]{1,0:T(8,128)(2,1)S(1)}, bf16[416,256]{1,0:T(8,128)(2,1)S(1)}, u32[]{:S(2)}, u32[]{:S(2)}) collective-permute-start(bf16[416,256]{1,0:T(8,128)(2,1)S(1)} %dynamic-slice_convert_fusion.1), channel_id=1, source_target_pairs={{0,2},{1,5},{2,0},{3,7},{4,6},{5,1},{6,4},{7,3},{8,10},{9,13},{10,... | collective-permute-start | bytes 638984 | tf_op jit(solution)/shard_map/ppermute | solution.py:182
  54.4 3.6 %collective-permute-done.13 = bf16[416,256]{1,0:T(8,128)(2,1)S(1)} collective-permute-done((bf16[416,256]{1,0:T(8,128)(2,1)S(1)}, bf16[416,256]{1,0:T(8,128)(2,1)S(1)}, u32[]{:S(2)}, u32[]{:S(2)}) %collective-permute-start.13) | collective-permute-done | bytes 213024 | tf_op jit(solution)/shard_map/ppermute | solution.py:182
  58.3 2.0 %collective-permute-done.5 = bf16[416,256]{1,0:T(8,128)(2,1)S(1)} collective-permute-done((bf16[416,256]{1,0:T(8,128)(2,1)S(1)}, bf16[416,256]{1,0:T(8,128)(2,1)S(1)}, u32[]{:S(2)}, u32[]{:S(2)}) %collective-permute-start.5) | collective-permute-done | bytes 213024 | tf_op jit(solution)/shard_map/ppermute | solution.py:182
  60.6 2.3 %collective-permute-done.14 = bf16[208,256]{1,0:T(8,128)(2,1)S(1)} collective-permute-done((bf16[208,256]{1,0:T(8,128)(2,1)S(1)}, bf16[208,256]{1,0:T(8,128)(2,1)S(1)}, u32[]{:S(2)}, u32[]{:S(2)}) %collective-permute-start.14) | collective-permute-done | bytes 106528 | tf_op jit(solution)/shard_map/ppermute | solution.py:182
  62.9 1.2 %collective-permute-start.15 = (bf16[104,256]{1,0:T(8,128)(2,1)S(1)}, bf16[104,256]{1,0:T(8,128)(2,1)S(1)}, u32[]{:S(2)}, u32[]{:S(2)}) collective-permute-start(bf16[104,256]{1,0:T(8,128)(2,1)S(1)} %dynamic-slice_convert_fusion.4), channel_id=1, source_target_pairs={{0,8},{1,9},{2,10},{3,11},{4,12},{5,13},{6,14},{7,15},{8,0},{9,1},... | collective-permute-start | bytes 159752 | tf_op jit(solution)/shard_map/ppermute | solution.py:182
  65.4 1.6 %collective-permute-start.7 = (bf16[104,256]{1,0:T(8,128)(2,1)S(1)}, bf16[104,256]{1,0:T(8,128)(2,1)S(1)}, u32[]{:S(2)}, u32[]{:S(2)}) collective-permute-start(bf16[104,256]{1,0:T(8,128)(2,1)S(1)} %dynamic-slice_convert_fusion.5), channel_id=1, source_target_pairs={{0,8},{1,9},{2,10},{3,11},{4,12},{5,13},{6,14},{7,15},{8,0},{9,1},... | collective-permute-start | bytes 159752 | tf_op jit(solution)/shard_map/ppermute | solution.py:182
  67.0 2.3 %collective-permute-done.15 = bf16[104,256]{1,0:T(8,128)(2,1)S(1)} collective-permute-done((bf16[104,256]{1,0:T(8,128)(2,1)S(1)}, bf16[104,256]{1,0:T(8,128)(2,1)S(1)}, u32[]{:S(2)}, u32[]{:S(2)}) %collective-permute-start.15) | collective-permute-done | bytes 53280 | tf_op jit(solution)/shard_map/ppermute | solution.py:182
  69.8 1.8 %collective-permute-done.7 = bf16[104,256]{1,0:T(8,128)(2,1)S(1)} collective-permute-done((bf16[104,256]{1,0:T(8,128)(2,1)S(1)}, bf16[104,256]{1,0:T(8,128)(2,1)S(1)}, u32[]{:S(2)}, u32[]{:S(2)}) %collective-permute-start.7) | collective-permute-done | bytes 53280 | tf_op jit(solution)/shard_map/ppermute | solution.py:182
  72.4 2.8 %collective-permute-done.16 = bf16[104,256]{1,0:T(8,128)(2,1)S(1)} collective-permute-done((bf16[104,256]{1,0:T(8,128)(2,1)S(1)}, bf16[104,256]{1,0:T(8,128)(2,1)S(1)}, u32[]{:S(2)}, u32[]{:S(2)}) %collective-permute-start.16) | collective-permute-done | bytes 53280 | tf_op jit(solution)/shard_map/ppermute | solution.py:182
  75.3 1.3 %collective-permute-done.8 = bf16[104,256]{1,0:T(8,128)(2,1)S(1)} collective-permute-done((bf16[104,256]{1,0:T(8,128)(2,1)S(1)}, bf16[104,256]{1,0:T(8,128)(2,1)S(1)}, u32[]{:S(2)}, u32[]{:S(2)}) %collective-permute-start.8) | collective-permute-done | bytes 53280 | tf_op jit(solution)/shard_map/ppermute | solution.py:182
  76.7 1.4 %collective-permute-start.9 = (bf16[208,256]{1,0:T(8,128)(2,1)S(1)}, bf16[208,256]{1,0:T(8,128)(2,1)S(1)}, u32[]{:S(2)}, u32[]{:S(2)}) collective-permute-start(bf16[208,256]{1,0:T(8,128)(2,1)S(1)} %maximum_select_fusion.6), channel_id=1, source_target_pairs={{0,4},{1,3},{2,6},{3,1},{4,0},{5,7},{6,2},{7,5},{8,12},{9,11},{10,... | collective-permute-start | bytes 319496 | tf_op jit(solution)/shard_map/ppermute | solution.py:182
  78.1 3.1 %collective-permute-done.17 = bf16[208,256]{1,0:T(8,128)(2,1)S(1)} collective-permute-done((bf16[208,256]{1,0:T(8,128)(2,1)S(1)}, bf16[208,256]{1,0:T(8,128)(2,1)S(1)}, u32[]{:S(2)}, u32[]{:S(2)}) %collective-permute-start.17) | collective-permute-done | bytes 106528 | tf_op jit(solution)/shard_map/ppermute | solution.py:182
  81.5 4.4 %collective-permute-start.2 = (bf16[256,512]{1,0:T(8,128)(2,1)S(1)}, bf16[256,512]{1,0:T(8,128)(2,1)S(1)}, u32[]{:S(2)}, u32[]{:S(2)}) collective-permute-start(bf16[256,512]{1,0:T(8,128)(2,1)S(1)} %get-tuple-element.28), channel_id=1, source_target_pairs={{0,15},{1,0},{2,1},{3,2},{4,3},{5,4},{6,5},{7,6},{8,7},{9,8},{10,9... | collective-permute-start | bytes 786440 | tf_op jit(solution)/shard_map/ppermute | solution.py:182
  87.4 1.7 %convolution_convert_fusion = bf16[1024,512]{1,0:T(8,128)(2,1)} fusion(bf16[512,512]{1,0:T(8,128)(2,1)S(1)} %copy-done.15, bf16[1024,256]{1,0:T(8,128)(2,1)S(1)} %copy-done.20, bf16[1024,256]{1,0:T(8,128)(2,1)S(1)} %get-tuple-element.19), kind=kOutput, calls=%fused_computation.1 | convolution fusion | flops 539492352 | bytes 2621440 | tf_op jit(solution)/shard_map/dot_general | solution.py:19
  89.1 5.9 %collective-permute-done.10 = bf16[416,256]{1,0:T(8,128)(2,1)S(1)} collective-permute-done((bf16[416,256]{1,0:T(8,128)(2,1)S(1)}, bf16[416,256]{1,0:T(8,128)(2,1)S(1)}, u32[]{:S(2)}, u32[]{:S(2)}) %collective-permute-start.10) | collective-permute-done | bytes 213024 | tf_op jit(solution)/shard_map/ppermute | solution.py:182
  99.0 1.7 %fusion.7 = (f32[512,512]{1,0:T(8,128)}, f32[512,512]{1,0:T(8,128)}, f32[512,512]{1,0:T(8,128)}) fusion(f32[1664,512]{1,0:T(8,128)S(1)} %maximum_convert_fusion), kind=kLoop, calls=%fused_computation.41 | loop fusion | bytes 6291456 | tf_op jit(solution)/shard_map/slice | solution.py:261
  (101 shorter events, 24.2 us)
Async XLA Ops:
  0.6 20.5 %collective-permute-start = (bf16[256,512]{1,0:T(8,128)(2,1)}, bf16[256,512]{1,0:T(8,128)(2,1)}, u32[]{:S(2)}, u32[]{:S(2)}) collective-permute-start(bf16[256,512]{1,0:T(8,128)(2,1)} %own.3), channel_id=1, source_target_pairs={{0,1},{1,2},{2,3},{3,4},{4,5},{5,6},{6,7},{7,8},{8,9},{9,10},{10,1... | collective-permute-start | bytes 786440 | tf_op jit(solution)/shard_map/ppermute | solution.py:182
  1.1 20.0 %collective-permute-start.1 = (bf16[256,512]{1,0:T(8,128)(2,1)}, bf16[256,512]{1,0:T(8,128)(2,1)}, u32[]{:S(2)}, u32[]{:S(2)}) collective-permute-start(bf16[256,512]{1,0:T(8,128)(2,1)} %own.3), channel_id=1, source_target_pairs={{0,15},{1,0},{2,1},{3,2},{4,3},{5,4},{6,5},{7,6},{8,7},{9,8},{10,9... | collective-permute-start | bytes 786440 | tf_op jit(solution)/shard_map/ppermute | solution.py:182
  16.0 5.1 %copy-start.9 = (bf16[256,512]{1,0:T(8,128)(2,1)S(1)}, bf16[256,512]{1,0:T(8,128)(2,1)}, u32[]{:S(2)}) copy-start(bf16[256,512]{1,0:T(8,128)(2,1)} %own.3) | copy-start | bytes 786436
  21.1 10.5 %copy-start.6 = (bf16[1024,512]{1,0:T(8,128)(2,1)}, bf16[1024,512]{1,0:T(8,128)(2,1)S(1)}, u32[]{:S(2)}) copy-start(bf16[1024,512]{1,0:T(8,128)(2,1)S(1)} %get-tuple-element.18.d_agg) | copy-start | bytes 3145732
  34.1 16.7 %collective-permute-start.12 = (bf16[832,256]{1,0:T(8,128)(2,1)}, bf16[832,256]{1,0:T(8,128)(2,1)}, u32[]{:S(2)}, u32[]{:S(2)}) collective-permute-start(bf16[832,256]{1,0:T(8,128)(2,1)} %constant_dynamic-slice_fusion), channel_id=1, source_target_pairs={{0,1},{1,0},{2,3},{3,2},{4,5},{5,4},{6,7},{7,6},{8,9},{9,8},{10,11... | collective-permute-start | bytes 1277960 | tf_op jit(solution)/shard_map/ppermute | solution.py:182
  49.8 2.4 %collective-permute-start.4 = (bf16[832,256]{1,0:T(8,128)(2,1)S(1)}, bf16[832,256]{1,0:T(8,128)(2,1)S(1)}, u32[]{:S(2)}, u32[]{:S(2)}) collective-permute-start(bf16[832,256]{1,0:T(8,128)(2,1)S(1)} %constant_dynamic-slice_fusion.1), channel_id=1, source_target_pairs={{0,1},{1,0},{2,3},{3,2},{4,5},{5,4},{6,7},{7,6},{8,9},{9,8},{10,11... | collective-permute-start | bytes 1277960 | tf_op jit(solution)/shard_map/ppermute | solution.py:182
  52.1 5.9 %collective-permute-start.13 = (bf16[416,256]{1,0:T(8,128)(2,1)S(1)}, bf16[416,256]{1,0:T(8,128)(2,1)S(1)}, u32[]{:S(2)}, u32[]{:S(2)}) collective-permute-start(bf16[416,256]{1,0:T(8,128)(2,1)S(1)} %dynamic-slice_convert_fusion), channel_id=1, source_target_pairs={{0,2},{1,5},{2,0},{3,7},{4,6},{5,1},{6,4},{7,3},{8,10},{9,13},{10,... | collective-permute-start | bytes 638984 | tf_op jit(solution)/shard_map/ppermute | solution.py:182
  52.4 8.0 %collective-permute-start.5 = (bf16[416,256]{1,0:T(8,128)(2,1)S(1)}, bf16[416,256]{1,0:T(8,128)(2,1)S(1)}, u32[]{:S(2)}, u32[]{:S(2)}) collective-permute-start(bf16[416,256]{1,0:T(8,128)(2,1)S(1)} %dynamic-slice_convert_fusion.1), channel_id=1, source_target_pairs={{0,2},{1,5},{2,0},{3,7},{4,6},{5,1},{6,4},{7,3},{8,10},{9,13},{10,... | collective-permute-start | bytes 638984 | tf_op jit(solution)/shard_map/ppermute | solution.py:182
  58.1 4.8 %collective-permute-start.14 = (bf16[208,256]{1,0:T(8,128)(2,1)S(1)}, bf16[208,256]{1,0:T(8,128)(2,1)S(1)}, u32[]{:S(2)}, u32[]{:S(2)}) collective-permute-start(bf16[208,256]{1,0:T(8,128)(2,1)S(1)} %dynamic-slice_convert_fusion.2), channel_id=1, source_target_pairs={{0,4},{1,3},{2,6},{3,1},{4,0},{5,7},{6,2},{7,5},{8,12},{9,11},{10,... | collective-permute-start | bytes 319496 | tf_op jit(solution)/shard_map/ppermute | solution.py:182
  60.4 4.9 %collective-permute-start.6 = (bf16[208,256]{1,0:T(8,128)(2,1)S(1)}, bf16[208,256]{1,0:T(8,128)(2,1)S(1)}, u32[]{:S(2)}, u32[]{:S(2)}) collective-permute-start(bf16[208,256]{1,0:T(8,128)(2,1)S(1)} %dynamic-slice_convert_fusion.3), channel_id=1, source_target_pairs={{0,4},{1,3},{2,6},{3,1},{4,0},{5,7},{6,2},{7,5},{8,12},{9,11},{10,... | collective-permute-start | bytes 319496 | tf_op jit(solution)/shard_map/ppermute | solution.py:182
  62.9 6.3 %collective-permute-start.15 = (bf16[104,256]{1,0:T(8,128)(2,1)S(1)}, bf16[104,256]{1,0:T(8,128)(2,1)S(1)}, u32[]{:S(2)}, u32[]{:S(2)}) collective-permute-start(bf16[104,256]{1,0:T(8,128)(2,1)S(1)} %dynamic-slice_convert_fusion.4), channel_id=1, source_target_pairs={{0,8},{1,9},{2,10},{3,11},{4,12},{5,13},{6,14},{7,15},{8,0},{9,1},... | collective-permute-start | bytes 159752 | tf_op jit(solution)/shard_map/ppermute | solution.py:182
  65.4 6.2 %collective-permute-start.7 = (bf16[104,256]{1,0:T(8,128)(2,1)S(1)}, bf16[104,256]{1,0:T(8,128)(2,1)S(1)}, u32[]{:S(2)}, u32[]{:S(2)}) collective-permute-start(bf16[104,256]{1,0:T(8,128)(2,1)S(1)} %dynamic-slice_convert_fusion.5), channel_id=1, source_target_pairs={{0,8},{1,9},{2,10},{3,11},{4,12},{5,13},{6,14},{7,15},{8,0},{9,1},... | collective-permute-start | bytes 159752 | tf_op jit(solution)/shard_map/ppermute | solution.py:182
  69.3 18.1 %copy-start.15 = (bf16[512,512]{1,0:T(8,128)(2,1)S(1)}, bf16[512,512]{1,0:T(8,128)(2,1)}, u32[]{:S(2)}) copy-start(bf16[512,512]{1,0:T(8,128)(2,1)} %w_dst.1) | copy-start | bytes 1572868
  69.3 18.1 %copy-start.20 = (bf16[1024,256]{1,0:T(8,128)(2,1)S(1)}, bf16[1024,256]{1,0:T(8,128)(2,1)}, u32[]{:S(2)}) copy-start(bf16[1024,256]{1,0:T(8,128)(2,1)} %copy-done.19) | copy-start | bytes 1572868
  69.3 5.9 %collective-permute-start.16 = (bf16[104,256]{1,0:T(8,128)(2,1)S(1)}, bf16[104,256]{1,0:T(8,128)(2,1)S(1)}, u32[]{:S(2)}, u32[]{:S(2)}) collective-permute-start(bf16[104,256]{1,0:T(8,128)(2,1)S(1)} %add_convert_fusion.2), channel_id=1, source_target_pairs={{0,8},{1,9},{2,10},{3,11},{4,12},{5,13},{6,14},{7,15},{8,0},{9,1},... | collective-permute-start | bytes 159752 | tf_op jit(solution)/shard_map/ppermute | solution.py:182
  71.6 5.1 %collective-permute-start.8 = (bf16[104,256]{1,0:T(8,128)(2,1)S(1)}, bf16[104,256]{1,0:T(8,128)(2,1)S(1)}, u32[]{:S(2)}, u32[]{:S(2)}) collective-permute-start(bf16[104,256]{1,0:T(8,128)(2,1)S(1)} %add_convert_fusion.3), channel_id=1, source_target_pairs={{0,8},{1,9},{2,10},{3,11},{4,12},{5,13},{6,14},{7,15},{8,0},{9,1},... | collective-permute-start | bytes 159752 | tf_op jit(solution)/shard_map/ppermute | solution.py:182
  75.3 5.9 %collective-permute-start.17 = (bf16[208,256]{1,0:T(8,128)(2,1)S(1)}, bf16[208,256]{1,0:T(8,128)(2,1)S(1)}, u32[]{:S(2)}, u32[]{:S(2)}) collective-permute-start(bf16[208,256]{1,0:T(8,128)(2,1)S(1)} %maximum_select_fusion.7), channel_id=1, source_target_pairs={{0,4},{1,3},{2,6},{3,1},{4,0},{5,7},{6,2},{7,5},{8,12},{9,11},{10,... | collective-permute-start | bytes 319496 | tf_op jit(solution)/shard_map/ppermute | solution.py:182
  76.7 9.2 %collective-permute-start.9 = (bf16[208,256]{1,0:T(8,128)(2,1)S(1)}, bf16[208,256]{1,0:T(8,128)(2,1)S(1)}, u32[]{:S(2)}, u32[]{:S(2)}) collective-permute-start(bf16[208,256]{1,0:T(8,128)(2,1)S(1)} %maximum_select_fusion.6), channel_id=1, source_target_pairs={{0,4},{1,3},{2,6},{3,1},{4,0},{5,7},{6,2},{7,5},{8,12},{9,11},{10,... | collective-permute-start | bytes 319496 | tf_op jit(solution)/shard_map/ppermute | solution.py:182
  81.2 5.9 %collective-permute-start.18 = (bf16[416,256]{1,0:T(8,128)(2,1)S(1)}, bf16[416,256]{1,0:T(8,128)(2,1)S(1)}, u32[]{:S(2)}, u32[]{:S(2)}) collective-permute-start(bf16[416,256]{1,0:T(8,128)(2,1)S(1)} %maximum_select_fusion.5), channel_id=1, source_target_pairs={{0,2},{1,5},{2,0},{3,7},{4,6},{5,1},{6,4},{7,3},{8,10},{9,13},{10,... | collective-permute-start | bytes 638984 | tf_op jit(solution)/shard_map/ppermute | solution.py:182
  81.4 13.9 %collective-permute-start.3 = (bf16[256,512]{1,0:T(8,128)(2,1)S(1)}, bf16[256,512]{1,0:T(8,128)(2,1)S(1)}, u32[]{:S(2)}, u32[]{:S(2)}) collective-permute-start(bf16[256,512]{1,0:T(8,128)(2,1)S(1)} %get-tuple-element.29), channel_id=1, source_target_pairs={{0,1},{1,2},{2,3},{3,4},{4,5},{5,6},{6,7},{7,8},{8,9},{9,10},{10,1... | collective-permute-start | bytes 786440 | tf_op jit(solution)/shard_map/ppermute | solution.py:182
  81.5 13.8 %collective-permute-start.2 = (bf16[256,512]{1,0:T(8,128)(2,1)S(1)}, bf16[256,512]{1,0:T(8,128)(2,1)S(1)}, u32[]{:S(2)}, u32[]{:S(2)}) collective-permute-start(bf16[256,512]{1,0:T(8,128)(2,1)S(1)} %get-tuple-element.28), channel_id=1, source_target_pairs={{0,15},{1,0},{2,1},{3,2},{4,3},{5,4},{6,5},{7,6},{8,7},{9,8},{10,9... | collective-permute-start | bytes 786440 | tf_op jit(solution)/shard_map/ppermute | solution.py:182
  86.0 9.0 %collective-permute-start.10 = (bf16[416,256]{1,0:T(8,128)(2,1)S(1)}, bf16[416,256]{1,0:T(8,128)(2,1)S(1)}, u32[]{:S(2)}, u32[]{:S(2)}) collective-permute-start(bf16[416,256]{1,0:T(8,128)(2,1)S(1)} %maximum_select_fusion.4), channel_id=1, source_target_pairs={{0,2},{1,5},{2,0},{3,7},{4,6},{5,1},{6,4},{7,3},{8,10},{9,13},{10,... | collective-permute-start | bytes 638984 | tf_op jit(solution)/shard_map/ppermute | solution.py:182
  87.3 9.1 %collective-permute-start.19 = (bf16[832,256]{1,0:T(8,128)(2,1)S(1)}, bf16[832,256]{1,0:T(8,128)(2,1)S(1)}, u32[]{:S(2)}, u32[]{:S(2)}) collective-permute-start(bf16[832,256]{1,0:T(8,128)(2,1)S(1)} %maximum_select_fusion.3), channel_id=1, source_target_pairs={{0,1},{1,0},{2,3},{3,2},{4,5},{5,4},{6,7},{7,6},{8,9},{9,8},{10,11... | collective-permute-start | bytes 1277960 | tf_op jit(solution)/shard_map/ppermute | solution.py:182
  95.2 1.8 %collective-permute-start.11 = (bf16[832,256]{1,0:T(8,128)(2,1)S(1)}, bf16[832,256]{1,0:T(8,128)(2,1)S(1)}, u32[]{:S(2)}, u32[]{:S(2)}) collective-permute-start(bf16[832,256]{1,0:T(8,128)(2,1)S(1)} %maximum_select_fusion.2), channel_id=1, source_target_pairs={{0,1},{1,0},{2,3},{3,2},{4,5},{5,4},{6,7},{7,6},{8,9},{9,8},{10,11... | collective-permute-start | bytes 1277960 | tf_op jit(solution)/shard_map/ppermute | solution.py:182
  (18 other events, 32.4 us)

commit v2 on v1

v2 whole, which is shorter than its diff:
```python
import functools

import jax
import jax.numpy as jnp
from jax import lax
from jax.experimental import pallas as pl
from jax.experimental.pallas import tpu as pltpu
from jax.sharding import PartitionSpec as P

BF16 = jnp.bfloat16
F32 = jnp.float32
BASE_TILE = 256
TILE = 512
NT = (((1,), (1,)), ((), ()))
TN = (((0,), (0,)), ((), ()))
VMEM_LIMIT = 60 * 1024 * 1024
HBM = pl.BlockSpec(memory_space=pltpu.HBM)
VMEM = pl.BlockSpec(memory_space=pltpu.VMEM)


def dot(a, b, dims=(((1,), (0,)), ((), ()))):
    return lax.dot_general(a, b, dims, preferred_element_type=F32)


def params():
    return pltpu.CompilerParams(vmem_limit_bytes=VMEM_LIMIT)


def copies(sems, pairs):
    made = [pltpu.make_async_copy(a, b, sems.at[i]) for i, (a, b) in enumerate(pairs)]
    for copy in made:
        copy.start()
    return made


def base_kernel(
    parts, tiles, edge_h, grid_h, cot_h, w_edge_h, w_dst_h, w_out_h, bias,
    planes_h, base_h, d_agg_h,
    edge, grid, cot, w_edge, w_dst, w_out, planes, base, d_agg, wide, node, sems, in_sems, out_sems,
):
    nodes, width = grid.shape
    fan = planes.shape[0]
    cols = width // parts
    rows = nodes // tiles
    chunk = wide.shape[2]
    arriving = []
    for i in range(tiles):
        e = slice(i * fan * rows, (i + 1) * fan * rows)
        g = slice(i * rows, (i + 1) * rows)
        arriving.append(
            copies(in_sems.at[i], ((edge_h.at[e, :], edge.at[e, :]), (grid_h.at[g, :], grid.at[g, :])))
        )
        if i == 0:
            weights = copies(
                sems, ((w_dst_h, w_dst), (w_edge_h, w_edge), (w_out_h, w_out), (cot_h, cot))
            )
    leaving = []
    for i in range(tiles):
        e = slice(i * fan * rows, (i + 1) * fan * rows)
        g = slice(i * rows, (i + 1) * rows)
        for copy in arriving[i]:
            copy.wait()
        for c in range(wide.shape[0]):
            wide[c] = edge[e, c * chunk : (c + 1) * chunk].astype(F32)
        for k in range(fan):
            for c in range(wide.shape[0]):
                piece = wide[c, pl.ds(k, rows, stride=fan), :]
                planes[k, g, c * chunk : (c + 1) * chunk] = piece.astype(BF16)
        if i == 0:
            for copy in weights:
                copy.wait()
        node[...] = dot(grid[g, :], w_dst[...]) + bias[...]
        product = dot(planes[:, g, :].reshape(fan * rows, width), w_edge[...])
        upstream = dot(cot[:, g], w_out[...], TN).astype(BF16)
        for h in range(parts):
            lanes = slice(h * cols, (h + 1) * cols)
            d_agg[h, g, :] = upstream[:, lanes]
            for k in range(fan):
                base[h, k, g, :] = product[k * rows : (k + 1) * rows, lanes] + node[:, lanes]
        leaving += copies(
            out_sems.at[i],
            (
                (planes.at[:, g, :], planes_h.at[:, g, :]),
                (base.at[:, :, g, :], base_h.at[:, :, g, :]),
                (d_agg.at[:, g, :], d_agg_h.at[:, g, :]),
            ),
        )
    for copy in leaving:
        copy.wait()


def base_call(parts, edge, grid, cot_t, w_edge, w_dst, w_out_t, bias):
    nodes, width = grid.shape
    fan = edge.shape[0] // nodes
    outs = cot_t.shape[0]
    cols = width // parts
    tiles = nodes // BASE_TILE
    results = (
        ((fan, nodes, width), BF16),
        ((parts, fan, nodes, cols), F32),
        ((parts, nodes, cols), BF16),
    )
    return pl.pallas_call(
        functools.partial(base_kernel, parts, tiles),
        in_specs=[HBM] * 6 + [VMEM],
        out_specs=[HBM] * 3,
        out_shape=[jax.ShapeDtypeStruct(*result) for result in results],
        scratch_shapes=[
            pltpu.VMEM(edge.shape, BF16),
            pltpu.VMEM(grid.shape, BF16),
            pltpu.VMEM((outs, nodes), BF16),
            pltpu.VMEM((width, width), BF16),
            pltpu.VMEM((width, width), BF16),
            pltpu.VMEM((outs, width), BF16),
        ]
        + [pltpu.VMEM(*result) for result in results]
        + [
            pltpu.VMEM((width // 128, fan * BASE_TILE, 128), F32),
            pltpu.VMEM((BASE_TILE, width), F32),
            pltpu.SemaphoreType.DMA((4,)),
            pltpu.SemaphoreType.DMA((tiles, 2)),
            pltpu.SemaphoreType.DMA((tiles, 3)),
        ],
        compiler_params=params(),
        name="base_terms",
    )(edge, grid, cot_t, w_edge, w_dst, w_out_t, bias)


def column_kernel(
    h, tiles, planes_h, base_h, d_agg_h, grid_h, cot_h, src, low_h, own_h, high_h, w_src_h,
    packed, d_node, sums,
    planes, base, d_agg, grid, cot, near_rows, w_src, proj, *rest,
):
    pick, pick_t, d_pre = rest[:tiles], rest[tiles : 2 * tiles], rest[2 * tiles : 3 * tiles]
    g_edge, g_dst, g_out, g_bias, acc, sems, tile_sems = rest[3 * tiles :]
    fan, nodes, width = planes.shape
    owned = own_h.shape[0]
    outs, cols = g_out.shape
    rows = nodes // tiles
    lanes = pl.ds(h * cols, cols)
    started = copies(
        sems,
        [(w_src_h.at[:, lanes], w_src)]
        + [(part, near_rows.at[j]) for j, part in enumerate((low_h, own_h, high_h))]
        + [(d_agg_h.at[h], d_agg), (cot_h, cot), (grid_h, grid)],
    )
    arriving = []
    for i in range(tiles):
        g = slice(i * rows, (i + 1) * rows)
        arriving.append(
            copies(
                tile_sems.at[i],
                (
                    (base_h.at[h, :, g, :], base.at[:, g, :]),
                    (planes_h.at[:, g, :], planes.at[:, g, :]),
                ),
            )
        )
    regions = lax.axis_size("region")
    first = (lax.axis_index("region") - 1) * owned
    one, zero = jnp.ones((), BF16), jnp.zeros((), BF16)
    across = lax.broadcasted_iota(jnp.int32, (rows, owned), 1).astype(F32).astype(BF16)
    down = lax.broadcasted_iota(jnp.int32, (owned, rows), 0).astype(F32).astype(BF16)

    def picks(i):
        local = src[:, i * rows : (i + 1) * rows] - first
        local = jnp.where(local < 0, local + owned * regions, local)
        local = jnp.where(local >= owned * regions, local - owned * regions, local).astype(F32)
        tall = jnp.transpose(jnp.concatenate([local, jnp.zeros((8 - fan, rows), F32)], axis=0))
        for k in range(fan):
            for j in range(3):
                place = (tall[:, k : k + 1] - float(j * owned)).astype(BF16)
                pick[i][k * rows : (k + 1) * rows, j * owned : (j + 1) * owned] = jnp.where(
                    across == place, one, zero
                )
                place = (local[k : k + 1, :] - float(j * owned)).astype(BF16)
                pick_t[i][j * owned : (j + 1) * owned, k * rows : (k + 1) * rows] = jnp.where(
                    down == place, one, zero
                )

    def add(total, i, term):
        if i == 0:
            total[...] = term
        else:
            total[...] += term

    picks(0)
    for copy in started[:4]:
        copy.wait()
    for j in range(3):
        proj[j * owned : (j + 1) * owned] = dot(near_rows[j], w_src[...]).astype(BF16)
    for copy in started[4:]:
        copy.wait()
    for i in range(tiles):
        g = slice(i * rows, (i + 1) * rows)
        for copy in arriving[i]:
            copy.wait()
        pre = base[:, g, :].reshape(fan * rows, cols) + dot(pick[i][...], proj[...])
        if i + 1 < tiles:
            picks(i + 1)
        upstream = d_agg[g, :].astype(F32)
        silu_sum = node_sum = None
        for k in range(fan):
            part = slice(k * rows, (k + 1) * rows)
            sig = 0.5 + 0.5 * jnp.tanh(0.5 * pre[part])
            silu = pre[part] * sig
            term = (upstream * (sig + silu * (1.0 - sig))).astype(BF16)
            d_pre[i][part] = term
            silu_sum = silu if k == 0 else silu_sum + silu
            node_sum = term.astype(F32) if k == 0 else node_sum + term.astype(F32)
        agg = silu_sum.astype(BF16)
        node = node_sum.astype(BF16)
        d_node[g, :] = node
        add(acc, i, dot(pick_t[i][...], d_pre[i][...]))
        add(g_edge, i, dot(planes[:, g, :].reshape(fan * rows, width), d_pre[i][...], TN))
        add(g_out, i, dot(cot[:, g], agg))
        add(g_dst, i, dot(grid[g, :], node, TN))
        add(g_bias, i, jnp.sum(node_sum.reshape(rows // 8, 8, cols), axis=0))
    total = acc[...].astype(BF16)
    sums[...] = total
    near_all = near_rows[...].reshape(3 * owned, width)
    packed[0:width] = dot(near_all, total, TN).astype(BF16)
    packed[width : 2 * width] = g_edge[...].astype(BF16)
    packed[2 * width : 3 * width] = g_dst[...].astype(BF16)
    tail = packed.shape[0] - 3 * width
    bias_row = jnp.sum(g_bias[...], axis=0, keepdims=True)
    place = lax.broadcasted_iota(jnp.int32, (tail, cols), 0)
    out_rows = jnp.concatenate([g_out[...], jnp.zeros((tail - outs, cols), F32)], axis=0)
    packed[3 * width :] = jnp.where(place == outs, bias_row, out_rows).astype(BF16)


def column_call(h, parts, planes, base, d_agg, grid, cot_t, src_t, low, own, high, w_src, rows):
    fan, nodes, width = planes.shape
    cols = width // parts
    outs = cot_t.shape[0]
    owned = own.shape[0]
    near = 3 * owned
    tiles = nodes // TILE
    return pl.pallas_call(
        functools.partial(column_kernel, h, tiles),
        in_specs=[HBM] * 5 + [VMEM] + [HBM] * 4,
        out_specs=[VMEM] * 3,
        out_shape=[
            jax.ShapeDtypeStruct((rows, cols), BF16),
            jax.ShapeDtypeStruct((nodes, cols), BF16),
            jax.ShapeDtypeStruct((near, cols), BF16),
        ],
        scratch_shapes=[
            pltpu.VMEM((fan, nodes, width), BF16),
            pltpu.VMEM((fan, nodes, cols), F32),
            pltpu.VMEM((nodes, cols), BF16),
            pltpu.VMEM((nodes, width), BF16),
            pltpu.VMEM((outs, nodes), BF16),
            pltpu.VMEM((3, owned, width), BF16),
            pltpu.VMEM((width, cols), BF16),
            pltpu.VMEM((near, cols), BF16),
        ]
        + [pltpu.VMEM((fan * TILE, near), BF16)] * tiles
        + [pltpu.VMEM((near, fan * TILE), BF16)] * tiles
        + [pltpu.VMEM((fan * TILE, cols), BF16)] * tiles
        + [
            pltpu.VMEM((width, cols), F32),
            pltpu.VMEM((width, cols), F32),
            pltpu.VMEM((outs, cols), F32),
            pltpu.VMEM((8, cols), F32),
            pltpu.VMEM((near, cols), F32),
            pltpu.SemaphoreType.DMA((7,)),
            pltpu.SemaphoreType.DMA((tiles, 2)),
        ],
        compiler_params=params(),
        name=f"columns_{h}",
    )(planes, base, d_agg, grid, cot_t, src_t, low, own, high, w_src)


def exchanged(block, partner_of):
    regions = lax.axis_size("region")
    return lax.ppermute(block, "region", [(i, partner_of(i)) for i in range(regions)])


def orders(regions):
    bits = [1 << b for b in range(1, regions.bit_length() - 1)]
    other = list(bits)
    if len(other) > 1:
        other[0], other[1] = other[1], other[0]
    return [1] + bits, [1] + other


def total_over_regions(block):
    regions = lax.axis_size("region")
    here = lax.axis_index("region")
    even, odd = orders(regions)
    stages = []
    for a, b in zip(even, odd):
        side = jnp.where(here % 2 == 0, (here // a) % 2, (here // b) % 2)
        stages.append((side, lambda i, a=a, b=b: i ^ (b if i % 2 else a)))
    last_side, last_partner = stages.pop()
    for side, partner in stages:
        half = block.shape[0] // 2
        send = lax.dynamic_slice_in_dim(block, (1 - side) * half, half, 0).astype(BF16)
        arrived = exchanged(send, partner)
        keep = lax.dynamic_slice_in_dim(block, side * half, half, 0)
        block = keep.astype(F32) + arrived.astype(F32)
    block = block.astype(BF16)
    block = (block.astype(F32) + exchanged(block, last_partner).astype(F32)).astype(BF16)
    for side, partner in reversed(stages):
        arrived = exchanged(block, partner)
        block = jnp.where(
            side == 0, jnp.concatenate([block, arrived]), jnp.concatenate([arrived, block])
        )
    return block


def ring(regions, distance):
    return lambda i: (i + distance) % regions


def shards(
    grid_latent, edge_latent, mesh_latent, sources, w_src, w_edge, w_dst, bias, w_out, cotangent
):
    owned, width = mesh_latent.shape
    outs = cotangent.shape[1]
    regions = lax.axis_size("region")
    low = exchanged(mesh_latent, ring(regions, 1))
    high = exchanged(mesh_latent, ring(regions, -1))
    cot_t, src_t = cotangent.T, sources.T
    parts = 2
    planes, base, d_agg = base_call(
        parts, edge_latent, grid_latent, cot_t, w_edge, w_dst, w_out.T, bias.reshape(1, -1)
    )
    unit = 8 * regions
    rows = -(-(3 * width + outs + 1) // unit) * unit
    packed, d_node, sums = [], [], []
    for h in range(parts):
        a, b, c = column_call(
            h, parts, planes, base, d_agg, grid_latent, cot_t, src_t,
            low, mesh_latent, high, w_src, rows,
        )
        packed.append(a)
        d_node.append(b)
        sums.append(c)
    totals = [total_over_regions(block) for block in packed]
    sums = jnp.concatenate(sums, axis=1)
    d_mesh_in = (
        sums[owned : 2 * owned].astype(F32)
        + exchanged(sums[:owned], ring(regions, -1)).astype(F32)
        + exchanged(sums[2 * owned :], ring(regions, 1)).astype(F32)
    ).astype(BF16)
    d_mesh = dot(d_mesh_in, w_src, NT)
    d_grid = dot(jnp.concatenate(d_node, axis=1), w_dst, NT).astype(BF16)
    total = jnp.concatenate(totals, axis=1).astype(F32)
    return (
        d_grid,
        d_mesh,
        total[:width],
        total[width : 2 * width],
        total[2 * width : 3 * width],
        total[3 * width + outs],
        total[3 * width : 3 * width + outs].T,
    )


def solution(mesh):
    placed = (
        P(("member", "region"), None),
        P(("member", "region"), None),
        P(("member", "region"), None),
        P("region", None),
        P(),
        P(),
        P(),
        P(),
        P(),
        P(("member", "region"), None),
    )
    return jax.shard_map(
        shards,
        mesh=mesh,
        in_specs=placed,
        out_specs=(
            P(("member", "region"), None),
            P(("member", "region"), None),
            P("member", None),
            P("member", None),
            P("member", None),
            P("member"),
            P("member", None),
        ),
        check_vma=False,
    )
```

time: 101 us -> 86.3 us (0.85)
  local copies, waits for them, and re-layouts: 19.6 us -> 5.99 us
  Pallas kernels: 25.6 us -> 28.8 us
  starting transfers between devices: 19.2 us -> 17.1 us
  other arithmetic: 4.74 us -> 3.02 us
    unnamed x47 -> x19, local copies, waits for them, and re-layouts: 15.8 us -> 1.91 us
    pallas_call x3, Pallas kernels: 25.6 us -> 28.8 us  [the longest x2 21 us: column_call(): pl.pallas_call(functools.partial(column_kernel, h, tiles), in_specs=[HBM]...]
    ppermute x20 -> x18, starting transfers between devices: 19.2 us -> 17.1 us  [exchanged(): lax.ppermute(block, 'region', [(i, partner_of(i)) for i in range(regions)])]
    dynamic_slice x2, local copies, waits for them, and re-layouts: 0.82 us -> 2.18 us  [total_over_regions(): lax.dynamic_slice_in_dim(block, (1 - side) * half, half, 0).astype(BF16)]
    add x6 -> x4, other arithmetic: 1.31 us -> 0.26 us  [total_over_regions(): block = keep.astype(F32) + arrived.astype(F32)]
    select_n x1 -> x0, local copies, waits for them, and re-layouts: 1.02 us -> none  [shards(): local = jnp.mod(sources - (here - 1) * owned, owned * regions)]
    ppermute x20 -> x18, waiting for transfers between devices: 27.7 us -> 27.1 us  [exchanged(): lax.ppermute(block, 'region', [(i, partner_of(i)) for i in range(regions)])]
  transfers between devices with their start and end apart: 20 -> 18, of which waited for: 12 -> 10; matrix products, arithmetic and copies ran while one was open for 9% -> 7% of each run, Pallas kernels for 15% -> 21%
where the time goes in v2:
time: 86.3 us; the launch traced here: 86 us
  Pallas kernels  28.8 us (33%)
  waiting for transfers between devices  27.1 us (31%)
  starting transfers between devices  17.1 us (20%)
  local copies, waits for them, and re-layouts  5.99 us (7%)
  other arithmetic  3.02 us (3%)
  matrix products  2.85 us (3%)
  between operations  1.12 us (1%)
    ppermute x18, waiting for transfers between devices, exchanged(): lax.ppermute(block, 'region', [(i, partner_of(i)) for i in range(regions)])  27.1 us
    pallas_call x2, Pallas kernels, column_call(): pl.pallas_call(functools.partial(column_kernel, h, tiles), in_specs=[HBM]...  21 us
    ppermute x18, starting transfers between devices, exchanged(): lax.ppermute(block, 'region', [(i, partner_of(i)) for i in range(regions)])  17.1 us
    pallas_call x1, Pallas kernels, base_call(): pl.pallas_call(functools.partial(base_kernel, parts, tiles), in_specs=[HB...  7.83 us
    dot_general x2, matrix products, dot(): return lax.dot_general(a, b, dims, preferred_element_type=F32)  2.85 us
    dynamic_slice x2, local copies, waits for them, and re-layouts, total_over_regions(): lax.dynamic_slice_in_dim(block, (1 - side) * half, half, 0).astype(BF16)  2.18 us
    unnamed x19, local copies, waits for them, and re-layouts  1.91 us
    slice x1, local copies, waits for them, and re-layouts, shards(): total[2 * width:3 * width]  1.73 us
  transfers between devices with their start and end apart: 18, of which 10 were waited for; matrix products, arithmetic and copies ran while one was open for 7% of the time, Pallas kernels for 21%

profile of v2, /device:TPU:0, one launch (start us, length us, event | category | flops | bytes accessed | tf_op | source)
XLA Modules:
  0.0 86.0 jit_solution(17398027157313977167)
XLA Ops:
  1.1 5.1 %collective-permute-start.1 = (bf16[256,512]{1,0:T(8,128)(2,1)}, bf16[256,512]{1,0:T(8,128)(2,1)S(1)}, u32[]{:S(2)}, u32[]{:S(2)}) collective-permute-start(bf16[256,512]{1,0:T(8,128)(2,1)} %own_h.3), channel_id=1, source_target_pairs={{0,15},{1,0},{2,1},{3,2},{4,3},{5,4},{6,5},{7,6},{8,7},{9,8},{10,9... | collective-permute-start | bytes 786440 | tf_op jit(solution)/shard_map/ppermute | solution.py:277
  6.2 7.8 %base_terms.1 = (bf16[3,1024,512]{2,1,0:T(8,128)(2,1)}, f32[2,3,1024,256]{3,2,1,0:T(8,128)}, bf16[2,1024,256]{2,1,0:T(8,128)(2,1)}) custom-call(bf16[3072,512]{1,0:T(8,128)(2,1)} %edge_h.1, bf16[1024,512]{1,0:T(8,128)(2,1)} %grid_h.5, bf16[84,1024]{1,0:T(8,128)(2,1)} %bitcast.9, bf16[512,512]{1,0:T(8,128)(2,1)} %w_edge_h.1, bf16[512,512]{1,0:T(8,128)(2,1)} %w_dst_h.1, ...), custom_call_target="tpu_custom_call" | custom-call | tf_op jit(solution)/shard_map/base_terms/pallas_call | solution.py:103
  14.8 10.4 %columns_1.1 = (bf16[1664,256]{1,0:T(8,128)(2,1)}, bf16[1024,256]{1,0:T(8,128)(2,1)}, bf16[768,256]{1,0:T(8,128)(2,1)}) custom-call(bf16[3,1024,512]{2,1,0:T(8,128)(2,1)} %get-tuple-element.16.planes_h, f32[2,3,1024,256]{3,2,1,0:T(8,128)} %get-tuple-element.17.base_h, bf16[2,1024,256]{2,1,0:T(8,128)(2,1)} %get-tuple-element.18.d_agg_h, ...), custom_call_target="tpu_custom_call" | custom-call | tf_op jit(solution)/shard_map/columns_1/pallas_call | solution.py:239
  25.3 1.0 %constant_dynamic-slice_fusion = bf16[832,256]{1,0:T(8,128)(2,1)S(1)} fusion(bf16[1664,256]{1,0:T(8,128)(2,1)} %get-tuple-element.24, s32[]{:T(128)S(6)} %select_n.143), kind=kLoop, calls=%fused_computation.29 | loop fusion | bytes 851972 | tf_op jit(solution)/shard_map/dynamic_slice | solution.py:299
  26.5 10.6 %columns_0.1 = (bf16[1664,256]{1,0:T(8,128)(2,1)}, bf16[1024,256]{1,0:T(8,128)(2,1)}, bf16[768,256]{1,0:T(8,128)(2,1)}) custom-call(bf16[3,1024,512]{2,1,0:T(8,128)(2,1)} %get-tuple-element.16.planes_h, f32[2,3,1024,256]{3,2,1,0:T(8,128)} %get-tuple-element.17.base_h, bf16[2,1024,256]{2,1,0:T(8,128)(2,1)} %get-tuple-element.18.d_agg_h, ...), custom_call_target="tpu_custom_call" | custom-call | tf_op jit(solution)/shard_map/columns_0/pallas_call | solution.py:239
  37.1 1.1 %constant_dynamic-slice_fusion.1 = bf16[832,256]{1,0:T(8,128)(2,1)S(1)} fusion(bf16[1664,256]{1,0:T(8,128)(2,1)} %get-tuple-element.23, s32[]{:T(128)S(6)} %select_n.143), kind=kLoop, calls=%fused_computation.30 | loop fusion | bytes 851972 | tf_op jit(solution)/shard_map/dynamic_slice | solution.py:299
  38.7 1.1 %constant_dynamic-update-slice_fusion.1 = bf16[768,512]{1,0:T(8,128)(2,1)S(1)} fusion(bf16[768,256]{1,0:T(8,128)(2,1)} %get-tuple-element.21), kind=kLoop, calls=%fused_computation.28 | loop fusion | bytes 786432
  40.2 2.1 %collective-permute-start.5 = (bf16[416,256]{1,0:T(8,128)(2,1)S(1)}, bf16[416,256]{1,0:T(8,128)(2,1)S(1)}, u32[]{:S(2)}, u32[]{:S(2)}) collective-permute-start(bf16[416,256]{1,0:T(8,128)(2,1)S(1)} %dynamic-slice_convert_fusion.1), channel_id=1, source_target_pairs={{0,2},{1,5},{2,0},{3,7},{4,6},{5,1},{6,4},{7,3},{8,10},{9,13},{10,... | collective-permute-start | bytes 638984 | tf_op jit(solution)/shard_map/ppermute | solution.py:277
  42.3 3.6 %collective-permute-done.12 = bf16[416,256]{1,0:T(8,128)(2,1)S(1)} collective-permute-done((bf16[416,256]{1,0:T(8,128)(2,1)S(1)}, bf16[416,256]{1,0:T(8,128)(2,1)S(1)}, u32[]{:S(2)}, u32[]{:S(2)}) %collective-permute-start.12) | collective-permute-done | bytes 213024 | tf_op jit(solution)/shard_map/ppermute | solution.py:277
  46.2 2.2 %collective-permute-done.5 = bf16[416,256]{1,0:T(8,128)(2,1)S(1)} collective-permute-done((bf16[416,256]{1,0:T(8,128)(2,1)S(1)}, bf16[416,256]{1,0:T(8,128)(2,1)S(1)}, u32[]{:S(2)}, u32[]{:S(2)}) %collective-permute-start.5) | collective-permute-done | bytes 213024 | tf_op jit(solution)/shard_map/ppermute | solution.py:277
  48.6 2.2 %collective-permute-done.13 = bf16[208,256]{1,0:T(8,128)(2,1)S(1)} collective-permute-done((bf16[208,256]{1,0:T(8,128)(2,1)S(1)}, bf16[208,256]{1,0:T(8,128)(2,1)S(1)}, u32[]{:S(2)}, u32[]{:S(2)}) %collective-permute-start.13) | collective-permute-done | bytes 106528 | tf_op jit(solution)/shard_map/ppermute | solution.py:277
  50.8 1.2 %collective-permute-start.14 = (bf16[208,256]{1,0:T(8,128)(2,1)S(1)}, bf16[208,256]{1,0:T(8,128)(2,1)S(1)}, u32[]{:S(2)}, u32[]{:S(2)}) collective-permute-start(bf16[208,256]{1,0:T(8,128)(2,1)S(1)} %add_convert_fusion.3), channel_id=1, source_target_pairs={{0,8},{1,9},{2,10},{3,11},{4,12},{5,13},{6,14},{7,15},{8,0},{9,1},... | collective-permute-start | bytes 319496 | tf_op jit(solution)/shard_map/ppermute | solution.py:277
  52.0 1.8 %collective-permute-done.6 = bf16[208,256]{1,0:T(8,128)(2,1)S(1)} collective-permute-done((bf16[208,256]{1,0:T(8,128)(2,1)S(1)}, bf16[208,256]{1,0:T(8,128)(2,1)S(1)}, u32[]{:S(2)}, u32[]{:S(2)}) %collective-permute-start.6) | collective-permute-done | bytes 106528 | tf_op jit(solution)/shard_map/ppermute | solution.py:277
  53.9 1.4 %collective-permute-start.7 = (bf16[208,256]{1,0:T(8,128)(2,1)S(1)}, bf16[208,256]{1,0:T(8,128)(2,1)S(1)}, u32[]{:S(2)}, u32[]{:S(2)}) collective-permute-start(bf16[208,256]{1,0:T(8,128)(2,1)S(1)} %add_convert_fusion.5), channel_id=1, source_target_pairs={{0,8},{1,9},{2,10},{3,11},{4,12},{5,13},{6,14},{7,15},{8,0},{9,1},... | collective-permute-start | bytes 319496 | tf_op jit(solution)/shard_map/ppermute | solution.py:277
  55.3 5.2 %collective-permute-done.14 = bf16[208,256]{1,0:T(8,128)(2,1)S(1)} collective-permute-done((bf16[208,256]{1,0:T(8,128)(2,1)S(1)}, bf16[208,256]{1,0:T(8,128)(2,1)S(1)}, u32[]{:S(2)}, u32[]{:S(2)}) %collective-permute-start.14) | collective-permute-done | bytes 106528 | tf_op jit(solution)/shard_map/ppermute | solution.py:277
  60.6 1.0 %collective-permute-done.7 = bf16[208,256]{1,0:T(8,128)(2,1)S(1)} collective-permute-done((bf16[208,256]{1,0:T(8,128)(2,1)S(1)}, bf16[208,256]{1,0:T(8,128)(2,1)S(1)}, u32[]{:S(2)}, u32[]{:S(2)}) %collective-permute-start.7) | collective-permute-done | bytes 106528 | tf_op jit(solution)/shard_map/ppermute | solution.py:277
  61.6 1.1 %collective-permute-start.8 = (bf16[208,256]{1,0:T(8,128)(2,1)S(1)}, bf16[208,256]{1,0:T(8,128)(2,1)S(1)}, u32[]{:S(2)}, u32[]{:S(2)}) collective-permute-start(bf16[208,256]{1,0:T(8,128)(2,1)S(1)} %add_convert_fusion.4), channel_id=1, source_target_pairs={{0,4},{1,3},{2,6},{3,1},{4,0},{5,7},{6,2},{7,5},{8,12},{9,11},{10,... | collective-permute-start | bytes 319496 | tf_op jit(solution)/shard_map/ppermute | solution.py:277
  62.7 3.7 %collective-permute-done.15 = bf16[208,256]{1,0:T(8,128)(2,1)S(1)} collective-permute-done((bf16[208,256]{1,0:T(8,128)(2,1)S(1)}, bf16[208,256]{1,0:T(8,128)(2,1)S(1)}, u32[]{:S(2)}, u32[]{:S(2)}) %collective-permute-start.15) | collective-permute-done | bytes 106528 | tf_op jit(solution)/shard_map/ppermute | solution.py:277
  66.6 4.4 %collective-permute-start.2 = (bf16[256,512]{1,0:T(8,128)(2,1)S(1)}, bf16[256,512]{1,0:T(8,128)(2,1)S(1)}, u32[]{:S(2)}, u32[]{:S(2)}) collective-permute-start(bf16[256,512]{1,0:T(8,128)(2,1)S(1)} %get-tuple-element.28), channel_id=1, source_target_pairs={{0,15},{1,0},{2,1},{3,2},{4,3},{5,4},{6,5},{7,6},{8,7},{9,8},{10,9... | collective-permute-start | bytes 786440 | tf_op jit(solution)/shard_map/ppermute | solution.py:277
  71.2 1.1 %collective-permute-done.16 = bf16[416,256]{1,0:T(8,128)(2,1)S(1)} collective-permute-done((bf16[416,256]{1,0:T(8,128)(2,1)S(1)}, bf16[416,256]{1,0:T(8,128)(2,1)S(1)}, u32[]{:S(2)}, u32[]{:S(2)}) %collective-permute-start.16) | collective-permute-done | bytes 213024 | tf_op jit(solution)/shard_map/ppermute | solution.py:277
  72.7 1.7 %convolution_convert_fusion = bf16[1024,512]{1,0:T(8,128)(2,1)} fusion(bf16[512,512]{1,0:T(8,128)(2,1)S(1)} %copy-done.5, bf16[1024,256]{1,0:T(8,128)(2,1)S(1)} %copy-done.7, bf16[1024,256]{1,0:T(8,128)(2,1)S(1)} %copy-done.8), kind=kOutput, calls=%fused_computation.1 | convolution fusion | flops 539492352 | bytes 2621440 | tf_op jit(solution)/shard_map/dot_general | solution.py:22
  74.4 5.9 %collective-permute-done.9 = bf16[416,256]{1,0:T(8,128)(2,1)S(1)} collective-permute-done((bf16[416,256]{1,0:T(8,128)(2,1)S(1)}, bf16[416,256]{1,0:T(8,128)(2,1)S(1)}, u32[]{:S(2)}, u32[]{:S(2)}) %collective-permute-start.9) | collective-permute-done | bytes 213024 | tf_op jit(solution)/shard_map/ppermute | solution.py:277
  80.5 1.1 %fusion.3 = f32[256,512]{1,0:T(8,128)} fusion(bf16[512,512]{1,0:T(8,128)(2,1)S(1)} %copy-done, bf16[256,512]{1,0:T(8,128)(2,1)S(1)} %collective-permute-done.3, bf16[256,512]{1,0:T(8,128)(2,1)S(1)} %collective-permute-done.2, bf16[768,512]{1,0:T(8,128)(2,1)S(1)} %constant_dynamic-update-slice_fusion), kind=kOutput, calls=%fused_computation.16 | convolution fusion | flops 135004160 | bytes 1835008 | tf_op jit(solution)/shard_map/dot_general | solution.py:22
  84.2 1.7 %fusion.6 = (f32[512,512]{1,0:T(8,128)}, f32[512,512]{1,0:T(8,128)}, f32[512,512]{1,0:T(8,128)}) fusion(f32[1664,512]{1,0:T(8,128)S(1)} %maximum_convert_fusion), kind=kLoop, calls=%fused_computation.33 | loop fusion | bytes 6291456 | tf_op jit(solution)/shard_map/slice | solution.py:356
  (62 shorter events, 6.2 us)
Async XLA Ops:
  0.6 13.4 %collective-permute-start = (bf16[256,512]{1,0:T(8,128)(2,1)}, bf16[256,512]{1,0:T(8,128)(2,1)S(1)}, u32[]{:S(2)}, u32[]{:S(2)}) collective-permute-start(bf16[256,512]{1,0:T(8,128)(2,1)} %own_h.3), channel_id=1, source_target_pairs={{0,1},{1,2},{2,3},{3,4},{4,5},{5,6},{6,7},{7,8},{8,9},{9,10},{10,1... | collective-permute-start | bytes 786440 | tf_op jit(solution)/shard_map/ppermute | solution.py:277
  1.1 12.9 %collective-permute-start.1 = (bf16[256,512]{1,0:T(8,128)(2,1)}, bf16[256,512]{1,0:T(8,128)(2,1)S(1)}, u32[]{:S(2)}, u32[]{:S(2)}) collective-permute-start(bf16[256,512]{1,0:T(8,128)(2,1)} %own_h.3), channel_id=1, source_target_pairs={{0,15},{1,0},{2,1},{3,2},{4,3},{5,4},{6,5},{7,6},{8,7},{9,8},{10,9... | collective-permute-start | bytes 786440 | tf_op jit(solution)/shard_map/ppermute | solution.py:277
  26.3 13.5 %collective-permute-start.11 = (bf16[832,256]{1,0:T(8,128)(2,1)S(1)}, bf16[832,256]{1,0:T(8,128)(2,1)S(1)}, u32[]{:S(2)}, u32[]{:S(2)}) collective-permute-start(bf16[832,256]{1,0:T(8,128)(2,1)S(1)} %constant_dynamic-slice_fusion), channel_id=1, source_target_pairs={{0,1},{1,0},{2,3},{3,2},{4,5},{5,4},{6,7},{7,6},{8,9},{9,8},{10,11... | collective-permute-start | bytes 1277960 | tf_op jit(solution)/shard_map/ppermute | solution.py:277
  37.1 2.7 %copy-start.6 = (bf16[768,256]{1,0:T(8,128)(2,1)S(1)}, bf16[768,256]{1,0:T(8,128)(2,1)}, u32[]{:S(2)}) copy-start(bf16[768,256]{1,0:T(8,128)(2,1)} %get-tuple-element.22) | copy-start | bytes 1179652
  37.1 2.8 %copy-start.3 = (bf16[1664,256]{1,0:T(8,128)(2,1)S(1)}, bf16[1664,256]{1,0:T(8,128)(2,1)}, u32[]{:S(2)}) copy-start(bf16[1664,256]{1,0:T(8,128)(2,1)} %get-tuple-element.24) | copy-start | bytes 2555908
  38.2 1.9 %collective-permute-start.4 = (bf16[832,256]{1,0:T(8,128)(2,1)S(1)}, bf16[832,256]{1,0:T(8,128)(2,1)S(1)}, u32[]{:S(2)}, u32[]{:S(2)}) collective-permute-start(bf16[832,256]{1,0:T(8,128)(2,1)S(1)} %constant_dynamic-slice_fusion.1), channel_id=1, source_target_pairs={{0,1},{1,0},{2,3},{3,2},{4,5},{5,4},{6,7},{7,6},{8,9},{9,8},{10,11... | collective-permute-start | bytes 1277960 | tf_op jit(solution)/shard_map/ppermute | solution.py:277
  40.0 5.9 %collective-permute-start.12 = (bf16[416,256]{1,0:T(8,128)(2,1)S(1)}, bf16[416,256]{1,0:T(8,128)(2,1)S(1)}, u32[]{:S(2)}, u32[]{:S(2)}) collective-permute-start(bf16[416,256]{1,0:T(8,128)(2,1)S(1)} %dynamic-slice_convert_fusion), channel_id=1, source_target_pairs={{0,2},{1,5},{2,0},{3,7},{4,6},{5,1},{6,4},{7,3},{8,10},{9,13},{10,... | collective-permute-start | bytes 638984 | tf_op jit(solution)/shard_map/ppermute | solution.py:277
  40.2 8.2 %collective-permute-start.5 = (bf16[416,256]{1,0:T(8,128)(2,1)S(1)}, bf16[416,256]{1,0:T(8,128)(2,1)S(1)}, u32[]{:S(2)}, u32[]{:S(2)}) collective-permute-start(bf16[416,256]{1,0:T(8,128)(2,1)S(1)} %dynamic-slice_convert_fusion.1), channel_id=1, source_target_pairs={{0,2},{1,5},{2,0},{3,7},{4,6},{5,1},{6,4},{7,3},{8,10},{9,13},{10,... | collective-permute-start | bytes 638984 | tf_op jit(solution)/shard_map/ppermute | solution.py:277
  46.0 4.8 %collective-permute-start.13 = (bf16[208,256]{1,0:T(8,128)(2,1)S(1)}, bf16[208,256]{1,0:T(8,128)(2,1)S(1)}, u32[]{:S(2)}, u32[]{:S(2)}) collective-permute-start(bf16[208,256]{1,0:T(8,128)(2,1)S(1)} %dynamic-slice_convert_fusion.2), channel_id=1, source_target_pairs={{0,4},{1,3},{2,6},{3,1},{4,0},{5,7},{6,2},{7,5},{8,12},{9,11},{10,... | collective-permute-start | bytes 319496 | tf_op jit(solution)/shard_map/ppermute | solution.py:277
  48.5 5.4 %collective-permute-start.6 = (bf16[208,256]{1,0:T(8,128)(2,1)S(1)}, bf16[208,256]{1,0:T(8,128)(2,1)S(1)}, u32[]{:S(2)}, u32[]{:S(2)}) collective-permute-start(bf16[208,256]{1,0:T(8,128)(2,1)S(1)} %dynamic-slice_convert_fusion.3), channel_id=1, source_target_pairs={{0,4},{1,3},{2,6},{3,1},{4,0},{5,7},{6,2},{7,5},{8,12},{9,11},{10,... | collective-permute-start | bytes 319496 | tf_op jit(solution)/shard_map/ppermute | solution.py:277
  50.8 9.7 %collective-permute-start.14 = (bf16[208,256]{1,0:T(8,128)(2,1)S(1)}, bf16[208,256]{1,0:T(8,128)(2,1)S(1)}, u32[]{:S(2)}, u32[]{:S(2)}) collective-permute-start(bf16[208,256]{1,0:T(8,128)(2,1)S(1)} %add_convert_fusion.3), channel_id=1, source_target_pairs={{0,8},{1,9},{2,10},{3,11},{4,12},{5,13},{6,14},{7,15},{8,0},{9,1},... | collective-permute-start | bytes 319496 | tf_op jit(solution)/shard_map/ppermute | solution.py:277
  53.9 18.8 %copy-start.5 = (bf16[512,512]{1,0:T(8,128)(2,1)S(1)}, bf16[512,512]{1,0:T(8,128)(2,1)}, u32[]{:S(2)}) copy-start(bf16[512,512]{1,0:T(8,128)(2,1)} %w_dst_h.1) | copy-start | bytes 1572868
  53.9 18.8 %copy-start.7 = (bf16[1024,256]{1,0:T(8,128)(2,1)S(1)}, bf16[1024,256]{1,0:T(8,128)(2,1)}, u32[]{:S(2)}) copy-start(bf16[1024,256]{1,0:T(8,128)(2,1)} %get-tuple-element.20) | copy-start | bytes 1572868
  53.9 18.8 %copy-start.8 = (bf16[1024,256]{1,0:T(8,128)(2,1)S(1)}, bf16[1024,256]{1,0:T(8,128)(2,1)}, u32[]{:S(2)}) copy-start(bf16[1024,256]{1,0:T(8,128)(2,1)} %get-tuple-element.19) | copy-start | bytes 1572868
  53.9 7.7 %collective-permute-start.7 = (bf16[208,256]{1,0:T(8,128)(2,1)S(1)}, bf16[208,256]{1,0:T(8,128)(2,1)S(1)}, u32[]{:S(2)}, u32[]{:S(2)}) collective-permute-start(bf16[208,256]{1,0:T(8,128)(2,1)S(1)} %add_convert_fusion.5), channel_id=1, source_target_pairs={{0,8},{1,9},{2,10},{3,11},{4,12},{5,13},{6,14},{7,15},{8,0},{9,1},... | collective-permute-start | bytes 319496 | tf_op jit(solution)/shard_map/ppermute | solution.py:277
  60.5 5.9 %collective-permute-start.15 = (bf16[208,256]{1,0:T(8,128)(2,1)S(1)}, bf16[208,256]{1,0:T(8,128)(2,1)S(1)}, u32[]{:S(2)}, u32[]{:S(2)}) collective-permute-start(bf16[208,256]{1,0:T(8,128)(2,1)S(1)} %add_convert_fusion.2), channel_id=1, source_target_pairs={{0,4},{1,3},{2,6},{3,1},{4,0},{5,7},{6,2},{7,5},{8,12},{9,11},{10,... | collective-permute-start | bytes 319496 | tf_op jit(solution)/shard_map/ppermute | solution.py:277
  61.6 9.4 %collective-permute-start.8 = (bf16[208,256]{1,0:T(8,128)(2,1)S(1)}, bf16[208,256]{1,0:T(8,128)(2,1)S(1)}, u32[]{:S(2)}, u32[]{:S(2)}) collective-permute-start(bf16[208,256]{1,0:T(8,128)(2,1)S(1)} %add_convert_fusion.4), channel_id=1, source_target_pairs={{0,4},{1,3},{2,6},{3,1},{4,0},{5,7},{6,2},{7,5},{8,12},{9,11},{10,... | collective-permute-start | bytes 319496 | tf_op jit(solution)/shard_map/ppermute | solution.py:277
  66.4 5.9 %collective-permute-start.16 = (bf16[416,256]{1,0:T(8,128)(2,1)S(1)}, bf16[416,256]{1,0:T(8,128)(2,1)S(1)}, u32[]{:S(2)}, u32[]{:S(2)}) collective-permute-start(bf16[416,256]{1,0:T(8,128)(2,1)S(1)} %maximum_select_fusion.5), channel_id=1, source_target_pairs={{0,2},{1,5},{2,0},{3,7},{4,6},{5,1},{6,4},{7,3},{8,10},{9,13},{10,... | collective-permute-start | bytes 638984 | tf_op jit(solution)/shard_map/ppermute | solution.py:277
  66.6 13.9 %collective-permute-start.3 = (bf16[256,512]{1,0:T(8,128)(2,1)S(1)}, bf16[256,512]{1,0:T(8,128)(2,1)S(1)}, u32[]{:S(2)}, u32[]{:S(2)}) collective-permute-start(bf16[256,512]{1,0:T(8,128)(2,1)S(1)} %get-tuple-element.29), channel_id=1, source_target_pairs={{0,1},{1,2},{2,3},{3,4},{4,5},{5,6},{6,7},{7,8},{8,9},{9,10},{10,1... | collective-permute-start | bytes 786440 | tf_op jit(solution)/shard_map/ppermute | solution.py:277
  66.6 13.9 %collective-permute-start.2 = (bf16[256,512]{1,0:T(8,128)(2,1)S(1)}, bf16[256,512]{1,0:T(8,128)(2,1)S(1)}, u32[]{:S(2)}, u32[]{:S(2)}) collective-permute-start(bf16[256,512]{1,0:T(8,128)(2,1)S(1)} %get-tuple-element.28), channel_id=1, source_target_pairs={{0,15},{1,0},{2,1},{3,2},{4,3},{5,4},{6,5},{7,6},{8,7},{9,8},{10,9... | collective-permute-start | bytes 786440 | tf_op jit(solution)/shard_map/ppermute | solution.py:277
  71.1 9.1 %collective-permute-start.9 = (bf16[416,256]{1,0:T(8,128)(2,1)S(1)}, bf16[416,256]{1,0:T(8,128)(2,1)S(1)}, u32[]{:S(2)}, u32[]{:S(2)}) collective-permute-start(bf16[416,256]{1,0:T(8,128)(2,1)S(1)} %maximum_select_fusion.4), channel_id=1, source_target_pairs={{0,2},{1,5},{2,0},{3,7},{4,6},{5,1},{6,4},{7,3},{8,10},{9,13},{10,... | collective-permute-start | bytes 638984 | tf_op jit(solution)/shard_map/ppermute | solution.py:277
  72.5 9.1 %collective-permute-start.17 = (bf16[832,256]{1,0:T(8,128)(2,1)S(1)}, bf16[832,256]{1,0:T(8,128)(2,1)S(1)}, u32[]{:S(2)}, u32[]{:S(2)}) collective-permute-start(bf16[832,256]{1,0:T(8,128)(2,1)S(1)} %maximum_select_fusion.3), channel_id=1, source_target_pairs={{0,1},{1,0},{2,3},{3,2},{4,5},{5,4},{6,7},{7,6},{8,9},{9,8},{10,11... | collective-permute-start | bytes 1277960 | tf_op jit(solution)/shard_map/ppermute | solution.py:277
  72.6 7.9 %copy-start = (bf16[512,512]{1,0:T(8,128)(2,1)S(1)}, bf16[512,512]{1,0:T(8,128)(2,1)}, u32[]{:S(2)}) copy-start(bf16[512,512]{1,0:T(8,128)(2,1)} %w_src_h.3) | copy-start | bytes 1572868
  80.4 1.8 %collective-permute-start.10 = (bf16[832,256]{1,0:T(8,128)(2,1)S(1)}, bf16[832,256]{1,0:T(8,128)(2,1)S(1)}, u32[]{:S(2)}, u32[]{:S(2)}) collective-permute-start(bf16[832,256]{1,0:T(8,128)(2,1)S(1)} %maximum_select_fusion.2), channel_id=1, source_target_pairs={{0,1},{1,0},{2,3},{3,2},{4,5},{5,4},{6,7},{7,6},{8,9},{9,8},{10,11... | collective-permute-start | bytes 1277960 | tf_op jit(solution)/shard_map/ppermute | solution.py:277
  (3 other events, 2.9 us)

commit v3 on v0

v3 whole, which is shorter than its diff:
```python
import functools

import jax
import jax.numpy as jnp
from jax import lax
from jax.experimental import pallas as pl
from jax.experimental.pallas import tpu as pltpu
from jax.sharding import PartitionSpec as P

BF16 = jnp.bfloat16
F32 = jnp.float32
TILE = 512
NT = (((1,), (1,)), ((), ()))
TN = (((0,), (0,)), ((), ()))
VMEM_LIMIT = 60 * 1024 * 1024
HBM = pl.BlockSpec(memory_space=pltpu.HBM)
VMEM = pl.BlockSpec(memory_space=pltpu.VMEM)


def dot(a, b, dims=(((1,), (0,)), ((), ()))):
    return lax.dot_general(a, b, dims, preferred_element_type=F32)


def params():
    return pltpu.CompilerParams(vmem_limit_bytes=VMEM_LIMIT)


def copies(sems, pairs):
    made = [pltpu.make_async_copy(a, b, sems.at[i]) for i, (a, b) in enumerate(pairs)]
    for copy in made:
        copy.start()
    return made


def places(src, owned):
    regions = lax.axis_size("region")
    local = src - (lax.axis_index("region") - 1) * owned
    local = jnp.where(local < 0, local + owned * regions, local)
    return jnp.where(local >= owned * regions, local - owned * regions, local).astype(F32)


def one_hot(counter, place):
    return jnp.where(counter == place.astype(BF16), jnp.ones((), BF16), jnp.zeros((), BF16))


def counting(shape, dim):
    return lax.broadcasted_iota(jnp.int32, shape, dim).astype(F32).astype(BF16)


def edge_kernel(
    tiles, edge_h, grid_h, cot_h, src_h, own_h, chip_h, next_h, w_src_h, w_edge_h, w_dst_h, w_out_h, bias_h,
    send_a, keep_a, send_b, keep_b, own_sum_h, to_chip_h, to_next_h, d_node_h,
    edge, grid, cot, src, near_rows, w_src, w_dst, w_out, bias, rhs, wide, pre, node_term, d_pre, d_node, packed, sums, *rest,
):
    lhs, pick_t = rest[:tiles], rest[tiles : 2 * tiles]
    acc, g_edge, g_dst, g_out, g_bias, sems, near_sems, in_sems, out_sems = rest[2 * tiles :]
    nodes, width = grid.shape
    fan = src.shape[0]
    owned = own_h.shape[0]
    outs = cot.shape[0]
    rows = nodes // tiles
    chunk = wide.shape[2]
    regions = lax.axis_size("region")
    region = lax.axis_index("region")
    tile = [slice(i * rows, (i + 1) * rows) for i in range(tiles)]

    odd = region % 2
    arrived = copies(
        near_sems,
        [(own_h, near_rows.at[1]), (chip_h, near_rows.at[2 - 2 * odd]), (next_h, near_rows.at[2 * odd])],
    )
    started = copies(sems.at[0], [(src_h, src), (w_src_h, w_src)])
    arriving = []
    for i, g in enumerate(tile):
        e = slice(i * fan * rows, (i + 1) * fan * rows)
        arriving.append(
            copies(in_sems.at[i], ((edge_h.at[e, :], edge.at[e, :]), (grid_h.at[g, :], grid.at[g, :])))
        )
        if i == 0:
            weights = copies(
                sems.at[1],
                [(w_edge_h, rhs.at[:width, :]), (w_dst_h, w_dst), (w_out_h, w_out)]
                + [(cot_h, cot), (bias_h, bias)],
            )
    across = counting((rows, owned), 1)
    down = counting((owned, rows), 0)

    def picks(i):
        local = places(src[:, tile[i]], owned)
        tall = jnp.transpose(jnp.concatenate([local, jnp.zeros((8 - fan, rows), F32)], axis=0))
        for k in range(fan):
            for j in range(3):
                lanes = slice(width + j * owned, width + (j + 1) * owned)
                lhs[i][k * rows : (k + 1) * rows, lanes] = one_hot(
                    across, tall[:, k : k + 1] - float(j * owned)
                )

    def picks_t(i):
        local = places(src[:, tile[i]], owned)
        for k in range(fan):
            for j in range(3):
                pick_t[i][j * owned : (j + 1) * owned, k * rows : (k + 1) * rows] = one_hot(
                    down, local[k : k + 1, :] - float(j * owned)
                )

    def planes(i):
        e = slice(i * fan * rows, (i + 1) * fan * rows)
        for c in range(wide.shape[0]):
            wide[c] = edge[e, c * chunk : (c + 1) * chunk].astype(F32)
        for k in range(fan):
            for c in range(wide.shape[0]):
                piece = wide[c, pl.ds(k, rows, stride=fan), :]
                lhs[i][k * rows : (k + 1) * rows, c * chunk : (c + 1) * chunk] = piece.astype(BF16)

    def add(total, i, term):
        if i == 0:
            total[...] = term
        else:
            total[...] += term

    started[0].wait()
    for i in range(tiles):
        picks(i)
    started[1].wait()
    for copy in arrived:
        copy.wait()
    rhs[width:] = dot(near_rows[...].reshape(3 * owned, width), w_src[...]).astype(BF16)
    for i, g in enumerate(tile):
        for copy in arriving[i]:
            copy.wait()
        planes(i)
        if i == 0:
            for copy in weights:
                copy.wait()
        node_term[g, :] = dot(grid[g, :], w_dst[...]) + bias[...]
        pre[:, g, :] = dot(lhs[i][...], rhs[...]).reshape(fan, rows, width)
        picks_t(i)
    for i, g in enumerate(tile):
        upstream = dot(cot[:, g], w_out[...], TN).astype(BF16).astype(F32)
        silu_sum = node_sum = None
        for k in range(fan):
            value = pre[k, g, :] + node_term[g, :]
            sig = 0.5 + 0.5 * jnp.tanh(0.5 * value)
            silu = value * sig
            term = (upstream * (sig + silu * (1.0 - sig))).astype(BF16)
            d_pre[k, g, :] = term
            silu_sum = silu if k == 0 else silu_sum + silu
            node_sum = term.astype(F32) if k == 0 else node_sum + term.astype(F32)
        agg = silu_sum.astype(BF16)
        node = node_sum.astype(BF16)
        d_node[g, :] = node
        term = d_pre[:, g, :].reshape(fan * rows, width)
        add(acc, i, dot(pick_t[i][...], term))
        add(g_edge, i, dot(lhs[i][:, :width], term, TN))
        add(g_out, i, dot(cot[:, g], agg))
        add(g_dst, i, dot(grid[g, :], node, TN))
        add(g_bias, i, jnp.sum(node_sum.reshape(rows // 8, 8, width), axis=0))
    total = acc[...].astype(BF16)
    sums[...] = total.reshape(3, owned, width)
    tail = packed.shape[0] - 3 * width
    bias_row = jnp.sum(g_bias[...], axis=0, keepdims=True)
    place = lax.broadcasted_iota(jnp.int32, (tail, width), 0)
    out_rows = jnp.concatenate([g_out[...], jnp.zeros((tail - outs, width), F32)], axis=0)
    packed[:tail] = jnp.where(place == outs, bias_row, out_rows).astype(BF16)
    g_src = dot(near_rows[...].reshape(3 * owned, width), total, TN)
    packed[tail : tail + width] = g_src.astype(BF16)
    packed[tail + width : tail + 2 * width] = g_edge[...].astype(BF16)
    packed[tail + 2 * width :] = g_dst[...].astype(BF16)
    pairs = []
    start = 0
    for send, keep in ((send_a, keep_a), (send_b, keep_b)):
        half = send.shape[0]
        gone = pl.ds(pl.multiple_of(start + (1 - odd) * half, 8), half)
        kept = pl.ds(pl.multiple_of(start + odd * half, 8), half)
        pairs += [(packed.at[gone, :], send), (packed.at[kept, :], keep)]
        start += 2 * half
    pairs += [(sums.at[1], own_sum_h), (sums.at[2 - 2 * odd], to_chip_h)]
    pairs += [(sums.at[2 * odd], to_next_h), (d_node, d_node_h)]
    for copy in copies(out_sems, pairs):
        copy.wait()


def edge_call(edge, grid, cot_t, src_t, near, w_src, w_edge, w_dst, w_out_t, bias, chain_rows):
    nodes, width = grid.shape
    fan, outs = src_t.shape[0], cot_t.shape[0]
    owned = near[0].shape[0]
    reach = 3 * owned
    tiles = nodes // TILE
    halves = [rows // 2 for rows in chain_rows for _ in range(2)]
    shapes = [(rows, width) for rows in halves] + [(owned, width)] * 3 + [(nodes, width)]
    return pl.pallas_call(
        functools.partial(edge_kernel, tiles),
        in_specs=[HBM] * 12,
        out_specs=[HBM] * len(shapes),
        out_shape=[jax.ShapeDtypeStruct(shape, BF16) for shape in shapes],
        scratch_shapes=[
            pltpu.VMEM(edge.shape, BF16),
            pltpu.VMEM((nodes, width), BF16),
            pltpu.VMEM((outs, nodes), BF16),
            pltpu.VMEM((fan, nodes), jnp.int32),
            pltpu.VMEM((3, owned, width), BF16),
            pltpu.VMEM((width, width), BF16),
            pltpu.VMEM((width, width), BF16),
            pltpu.VMEM((outs, width), BF16),
            pltpu.VMEM((1, width), F32),
            pltpu.VMEM((width + reach, width), BF16),
            pltpu.VMEM((width // 128, fan * TILE, 128), F32),
            pltpu.VMEM((fan, nodes, width), F32),
            pltpu.VMEM((nodes, width), F32),
            pltpu.VMEM((fan, nodes, width), BF16),
            pltpu.VMEM((nodes, width), BF16),
            pltpu.VMEM((sum(chain_rows), width), BF16),
            pltpu.VMEM((3, owned, width), BF16),
        ]
        + [pltpu.VMEM((fan * TILE, width + reach), BF16)] * tiles
        + [pltpu.VMEM((reach, fan * TILE), BF16)] * tiles
        + [
            pltpu.VMEM((reach, width), F32),
            pltpu.VMEM((width, width), F32),
            pltpu.VMEM((width, width), F32),
            pltpu.VMEM((outs, width), F32),
            pltpu.VMEM((8, width), F32),
            pltpu.SemaphoreType.DMA((2, 5)),
            pltpu.SemaphoreType.DMA((3,)),
            pltpu.SemaphoreType.DMA((tiles, 2)),
            pltpu.SemaphoreType.DMA((8,)),
        ],
        compiler_params=params(),
        name="edge_terms",
    )(edge, grid, cot_t, src_t, *near, w_src, w_edge, w_dst, w_out_t, bias)


def exchanged(block, pairs):
    return lax.ppermute(block, "region", pairs)


def orders(regions):
    bits = [1 << b for b in range(1, regions.bit_length() - 1)]
    other = list(bits)
    if len(other) > 1:
        other[0], other[1] = other[1], other[0]
    return [1] + bits, [1] + other


def stages_of(regions, here):
    stages = []
    for a, b in zip(*orders(regions)):
        side = jnp.where(here % 2 == 0, (here // a) % 2, (here // b) % 2)
        stages.append((side, [(i, i ^ (b if i % 2 else a)) for i in range(regions)]))
    return stages


def neighbours(regions):
    chip = [(i, i ^ 1) for i in range(regions)]
    return chip, [(i, (i + (1 if i % 2 else -1)) % regions) for i in range(regions)]


def after(value, other):
    corner = other[(slice(0, 1),) * other.ndim].reshape((1,) * value.ndim)
    return value + jnp.minimum(jnp.abs(corner), 0).astype(value.dtype)


class Chain:
    def __init__(self, keep, send, stages):
        self.stages, self.level = stages, 0
        self.block, self.arrived = keep, exchanged(send, stages[0][1])

    def total(self):
        return self.block.astype(F32) + self.arrived.astype(F32)

    def halve(self):
        self.level += 1
        side, partner = self.stages[self.level]
        block = self.total()
        half = block.shape[0] // 2
        send = lax.dynamic_slice_in_dim(block, (1 - side) * half, half, 0).astype(BF16)
        self.block = lax.dynamic_slice_in_dim(block, side * half, half, 0)
        self.arrived = exchanged(send, partner)

    def swap(self, *others):
        self.level += 1
        block = self.total()
        for other in others:
            block = after(block, other)
        self.block = block.astype(BF16)
        self.arrived = exchanged(self.block, self.stages[self.level][1])

    def double(self, *others):
        if self.level == len(self.stages) - 1:
            self.block = self.total().astype(BF16)
        else:
            self.block = self.joined(0, 2 * self.block.shape[0])
        for other in others:
            self.block = after(self.block, other)
        self.level -= 1
        self.arrived = exchanged(self.block, self.stages[self.level][1])

    def joined(self, start, stop):
        low = jnp.concatenate([self.block, self.arrived])[start:stop]
        high = jnp.concatenate([self.arrived, self.block])[start:stop]
        return jnp.where(self.stages[self.level][0] == 0, low, high)


def shards(
    grid_latent, edge_latent, mesh_latent, sources, w_src, w_edge, w_dst, bias, w_out, cotangent
):
    width = mesh_latent.shape[1]
    outs = cotangent.shape[1]
    regions = lax.axis_size("region")
    chip, beyond = neighbours(regions)
    near = (mesh_latent, exchanged(mesh_latent, chip), exchanged(mesh_latent, beyond))
    unit = 4 * regions
    units = -(-(3 * width + outs + 1) // unit)
    chain_rows = [-(-units // 2) * unit, units // 2 * unit]
    stages = stages_of(regions, lax.axis_index("region"))
    send_a, keep_a, send_b, keep_b, own_sum, to_chip, to_next, d_node = edge_call(
        edge_latent, grid_latent, cotangent.T, sources.T, near,
        w_src, w_edge, w_dst, w_out.T, bias.reshape(1, -1), chain_rows,
    )
    a = Chain(keep_a, send_a, stages)
    b = Chain(keep_b, send_b, stages)
    for level in range(1, len(stages) - 1):
        a.halve()
        b.halve()
    a.swap()
    b.swap()
    from_next = exchanged(after(to_next, a.block), beyond)
    from_chip = exchanged(to_chip, chip)
    d_mesh_in = sum(x.astype(F32) for x in (own_sum, from_chip, from_next))
    d_mesh = dot(d_mesh_in.astype(BF16), w_src, NT)
    d_grid = dot(after(d_node, a.block), w_dst, NT).astype(BF16)
    a.double()
    b.double(d_grid)
    for level in range(2, len(stages) - 1):
        a.double()
        b.double(d_mesh)
    a.double()
    b.double()
    starts = [sum(chain_rows) - i * width for i in (3, 2, 1, 0)]

    def rows_of(start, stop):
        cut = chain_rows[0]
        parts = []
        if start < cut:
            parts.append(a.joined(start, min(stop, cut)))
        if stop > cut:
            parts.append(b.joined(max(start, cut) - cut, stop - cut))
        return jnp.concatenate(parts).astype(F32)

    return (
        d_grid,
        d_mesh,
        rows_of(starts[0], starts[1]),
        rows_of(starts[1], starts[2]),
        rows_of(starts[2], starts[3]),
        rows_of(outs, outs + 1)[0],
        rows_of(0, outs).T,
    )


def solution(mesh):
    placed = (
        P(("member", "region"), None),
        P(("member", "region"), None),
        P(("member", "region"), None),
        P("region", None),
        P(),
        P(),
        P(),
        P(),
        P(),
        P(("member", "region"), None),
    )
    return jax.shard_map(
        shards,
        mesh=mesh,
        in_specs=placed,
        out_specs=(
            P(("member", "region"), None),
            P(("member", "region"), None),
            P("member", None),
            P("member", None),
            P("member", None),
            P("member"),
            P("member", None),
        ),
        check_vma=False,
    )
```

time: 262 us -> 78.7 us (0.30)
  local copies, waits for them, and re-layouts: 81.4 us -> 2.51 us
  matrix products: 43.5 us -> 1.08 us
  other arithmetic: 45.5 us -> 7.72 us
  blocking collectives: 34.5 us -> 0 us
  Pallas kernels: 0 us -> 17.5 us
  starting transfers between devices: 6.37 us -> 21.6 us
  between operations: 14.1 us -> 2.96 us
  waiting for transfers between devices: 34.9 us -> 25.1 us
    reshape x6 -> x0, local copies, waits for them, and re-layouts: 44.5 us -> none  [the longest x1 10.8 us: shards(): jnp.repeat(d_agg.astype(jnp.float32), fan_in, axis=0) * slope]
    dot_general x10 -> x2, matrix products: 43.5 us -> 1.08 us  [dot(): return lax.dot_general(a, b, dims, preferred_element_type=F32)]
    psum x1 -> x0, waiting for transfers between devices: 34.9 us -> none  [shards(): lax.psum((grad_src, grad_edge, grad_dst, grad_bias, grad_out), 'region')]
    psum x1 -> x0, blocking collectives: 34.5 us -> none  [shards(): lax.psum((grad_src, grad_edge, grad_dst, grad_bias, grad_out), 'region')]
    ppermute x4 -> x18, waiting for transfers between devices: 0.01 us -> 25.1 us  [exchanged(): return lax.ppermute(block, 'region', pairs)]
    scatter-add x1 -> x0, other arithmetic: 20.4 us -> none  [shards(): nearby = jnp.zeros((3 * owned, width), jnp.float32).at[local].add(mesh_term)]
    reduce_sum x2 -> x0, other arithmetic: 18.9 us -> none  [the longest x1 9.44 us: shards(): jnp.sum((pre * sig).reshape(nodes, fan_in, width), axis=1)]
    pallas_call x0 -> x1, Pallas kernels: none -> 17.5 us  [edge_call(): pl.pallas_call(functools.partial(edge_kernel, tiles), in_specs=[HBM] * 12...]
  transfers between devices with their start and end apart: 5 -> 18, of which waited for: 1 -> 8; matrix products, arithmetic and copies ran while one was open for 32% -> 11% of each run, Pallas kernels for 0% -> 0%
where the time goes in v3:
time: 78.7 us; the launch traced here: 78.4 us
  waiting for transfers between devices  25.1 us (32%)
  starting transfers between devices  21.6 us (27%)
  Pallas kernels  17.5 us (22%)
  other arithmetic  7.72 us (10%)
  between operations  2.96 us (4%)
  local copies, waits for them, and re-layouts  2.51 us (3%)
  matrix products  1.08 us (1%)
    ppermute x18, waiting for transfers between devices, exchanged(): return lax.ppermute(block, 'region', pairs)  25.1 us
    ppermute x18, starting transfers between devices, exchanged(): return lax.ppermute(block, 'region', pairs)  21.6 us
    pallas_call x1, Pallas kernels, edge_call(): pl.pallas_call(functools.partial(edge_kernel, tiles), in_specs=[HBM] * 12...  17.5 us
    convert_element_type x3, other arithmetic, rows_of(): return jnp.concatenate(parts).astype(F32)  3.33 us
    add x4, other arithmetic, total(): return self.block.astype(F32) + self.arrived.astype(F32)  2.52 us
    slice x3, local copies, waits for them, and re-layouts, after(): corner = other[(slice(0, 1),) * other.ndim].reshape((1,) * value.ndim)  1.65 us
  transfers between devices with their start and end apart: 18, of which 8 were waited for; matrix products, arithmetic and copies ran while one was open for 11% of the time, Pallas kernels for 0%

profile of v3, /device:TPU:0, one launch (start us, length us, event | category | flops | bytes accessed | tf_op | source)
XLA Modules:
  0.0 78.4 jit_solution(14088832015293578306)
XLA Ops:
  1.2 5.7 %collective-permute-start.1 = (bf16[256,512]{1,0:T(8,128)(2,1)}, bf16[256,512]{1,0:T(8,128)(2,1)S(1)}, u32[]{:S(2)}, u32[]{:S(2)}) collective-permute-start(bf16[256,512]{1,0:T(8,128)(2,1)} %own_h.1), channel_id=1, source_target_pairs={{0,15},{1,2},{2,1},{3,4},{4,3},{5,6},{6,5},{7,8},{8,7},{9,10},{10,... | collective-permute-start | bytes 786440 | tf_op jit(solution)/shard_map/ppermute | solution.py:234
  6.8 4.3 %collective-permute-done.1.next_h = bf16[256,512]{1,0:T(8,128)(2,1)S(1)} collective-permute-done((bf16[256,512]{1,0:T(8,128)(2,1)}, bf16[256,512]{1,0:T(8,128)(2,1)S(1)}, u32[]{:S(2)}, u32[]{:S(2)}) %collective-permute-start.1) | collective-permute-done | bytes 262176 | tf_op jit(solution)/shard_map/ppermute | solution.py:234
  11.1 0.7 copy-done.5
  11.8 17.5 %edge_terms.1 = (bf16[416,512]{1,0:T(8,128)(2,1)}, bf16[416,512]{1,0:T(8,128)(2,1)}, bf16[416,512]{1,0:T(8,128)(2,1)}, bf16[416,512]{1,0:T(8,128)(2,1)}, bf16[25...) custom-call(bf16[3072,512]{1,0:T(8,128)(2,1)} %edge_h.1, ...), custom_call_target="tpu_custom_call" | custom-call | tf_op jit(solution)/shard_map/edge_terms/pallas_call | solution.py:191
  29.9 1.4 %collective-permute-done.2 = bf16[416,512]{1,0:T(8,128)(2,1)S(1)} collective-permute-done((bf16[416,512]{1,0:T(8,128)(2,1)}, bf16[416,512]{1,0:T(8,128)(2,1)S(1)}, u32[]{:S(2)}, u32[]{:S(2)}) %collective-permute-start.2) | collective-permute-done | bytes 426016 | tf_op jit(solution)/shard_map/ppermute | solution.py:234
  31.3 1.3 %convert_add_fusion.1 = f32[416,512]{1,0:T(8,128)S(1)} fusion(bf16[416,512]{1,0:T(8,128)(2,1)S(1)} %collective-permute-done.2, bf16[416,512]{1,0:T(8,128)(2,1)} %get-tuple-element.16), kind=kLoop, calls=%fused_computation.3 | loop fusion | flops 638976 | bytes 1703936 | tf_op jit(solution)/shard_map/add | solution.py:269
  32.7 1.5 %collective-permute-start.3 = (bf16[208,512]{1,0:T(8,128)(2,1)S(1)}, bf16[208,512]{1,0:T(8,128)(2,1)S(1)}, u32[]{:S(2)}, u32[]{:S(2)}) collective-permute-start(bf16[208,512]{1,0:T(8,128)(2,1)S(1)} %dynamic-slice_convert_fusion.1), channel_id=1, source_target_pairs={{0,2},{1,5},{2,0},{3,7},{4,6},{5,1},{6,4},{7,3},{8,10},{9,13},{10,... | collective-permute-start | bytes 638984 | tf_op jit(solution)/shard_map/ppermute | solution.py:234
  34.2 1.1 %convert_add_fusion = f32[416,512]{1,0:T(8,128)S(1)} fusion(bf16[416,512]{1,0:T(8,128)(2,1)S(1)} %collective-permute-done.11, bf16[416,512]{1,0:T(8,128)(2,1)} %get-tuple-element.21), kind=kLoop, calls=%fused_computation.2 | loop fusion | flops 638976 | bytes 1703936 | tf_op jit(solution)/shard_map/add | solution.py:269
  36.0 2.6 %collective-permute-done.3 = bf16[208,512]{1,0:T(8,128)(2,1)S(1)} collective-permute-done((bf16[208,512]{1,0:T(8,128)(2,1)S(1)}, bf16[208,512]{1,0:T(8,128)(2,1)S(1)}, u32[]{:S(2)}, u32[]{:S(2)}) %collective-permute-start.3) | collective-permute-done | bytes 213024 | tf_op jit(solution)/shard_map/ppermute | solution.py:234
  38.7 1.6 %collective-permute-start.4 = (bf16[104,512]{1,0:T(8,128)(2,1)S(1)}, bf16[104,512]{1,0:T(8,128)(2,1)S(1)}, u32[]{:S(2)}, u32[]{:S(2)}) collective-permute-start(bf16[104,512]{1,0:T(8,128)(2,1)S(1)} %dynamic-slice_convert_fusion.3), channel_id=1, source_target_pairs={{0,4},{1,3},{2,6},{3,1},{4,0},{5,7},{6,2},{7,5},{8,12},{9,11},{10,... | collective-permute-start | bytes 319496 | tf_op jit(solution)/shard_map/ppermute | solution.py:234
  40.4 1.5 %collective-permute-done.12 = bf16[208,512]{1,0:T(8,128)(2,1)S(1)} collective-permute-done((bf16[208,512]{1,0:T(8,128)(2,1)S(1)}, bf16[208,512]{1,0:T(8,128)(2,1)S(1)}, u32[]{:S(2)}, u32[]{:S(2)}) %collective-permute-start.12) | collective-permute-done | bytes 213024 | tf_op jit(solution)/shard_map/ppermute | solution.py:234
  42.0 1.5 %collective-permute-start.13 = (bf16[104,512]{1,0:T(8,128)(2,1)S(1)}, bf16[104,512]{1,0:T(8,128)(2,1)S(1)}, u32[]{:S(2)}, u32[]{:S(2)}) collective-permute-start(bf16[104,512]{1,0:T(8,128)(2,1)S(1)} %dynamic-slice_convert_fusion.2), channel_id=1, source_target_pairs={{0,4},{1,3},{2,6},{3,1},{4,0},{5,7},{6,2},{7,5},{8,12},{9,11},{10,... | collective-permute-start | bytes 319496 | tf_op jit(solution)/shard_map/ppermute | solution.py:234
  44.0 2.6 %collective-permute-start.7 = (bf16[104,512]{1,0:T(8,128)(2,1)S(1)}, bf16[104,512]{1,0:T(8,128)(2,1)S(1)}, u32[]{:S(2)}, u32[]{:S(2)}) collective-permute-start(bf16[104,512]{1,0:T(8,128)(2,1)S(1)} %add_convert_fusion.5), channel_id=1, source_target_pairs={{0,8},{1,9},{2,10},{3,11},{4,12},{5,13},{6,14},{7,15},{8,0},{9,1},... | collective-permute-start | bytes 319496 | tf_op jit(solution)/shard_map/ppermute | solution.py:234
  47.3 0.7 convolution_convert_fusion
  49.5 1.6 %collective-permute-start.14 = (bf16[104,512]{1,0:T(8,128)(2,1)S(1)}, bf16[104,512]{1,0:T(8,128)(2,1)S(1)}, u32[]{:S(2)}, u32[]{:S(2)}) collective-permute-start(bf16[104,512]{1,0:T(8,128)(2,1)S(1)} %add_convert_fusion.3), channel_id=1, source_target_pairs={{0,8},{1,9},{2,10},{3,11},{4,12},{5,13},{6,14},{7,15},{8,0},{9,1},... | collective-permute-start | bytes 319496 | tf_op jit(solution)/shard_map/ppermute | solution.py:234
  51.9 8.0 %collective-permute-done.14 = bf16[104,512]{1,0:T(8,128)(2,1)S(1)} collective-permute-done((bf16[104,512]{1,0:T(8,128)(2,1)S(1)}, bf16[104,512]{1,0:T(8,128)(2,1)S(1)}, u32[]{:S(2)}, u32[]{:S(2)}) %collective-permute-start.14) | collective-permute-done | bytes 106528 | tf_op jit(solution)/shard_map/ppermute | solution.py:234
  60.1 2.7 %collective-permute-start.9 = (bf16[208,512]{1,0:T(8,128)(2,1)S(1)}, bf16[208,512]{1,0:T(8,128)(2,1)S(1)}, u32[]{:S(2)}, u32[]{:S(2)}) collective-permute-start(bf16[208,512]{1,0:T(8,128)(2,1)S(1)} %maximum_select_fusion.2), channel_id=1, source_target_pairs={{0,2},{1,5},{2,0},{3,7},{4,6},{5,1},{6,4},{7,3},{8,10},{9,13},{10,... | collective-permute-start | bytes 638984 | tf_op jit(solution)/shard_map/ppermute | solution.py:234
  64.4 2.7 %collective-permute-done.9 = bf16[208,512]{1,0:T(8,128)(2,1)S(1)} collective-permute-done((bf16[208,512]{1,0:T(8,128)(2,1)S(1)}, bf16[208,512]{1,0:T(8,128)(2,1)S(1)}, u32[]{:S(2)}, u32[]{:S(2)}) %collective-permute-start.9) | collective-permute-done | bytes 213024 | tf_op jit(solution)/shard_map/ppermute | solution.py:234
  67.6 1.7 %collective-permute-start.16 = (bf16[208,512]{1,0:T(8,128)(2,1)S(1)}, bf16[208,512]{1,0:T(8,128)(2,1)S(1)}, u32[]{:S(2)}, u32[]{:S(2)}) collective-permute-start(bf16[208,512]{1,0:T(8,128)(2,1)S(1)} %fusion.7), channel_id=1, source_target_pairs={{0,2},{1,5},{2,0},{3,7},{4,6},{5,1},{6,4},{7,3},{8,10},{9,13},{10,... | collective-permute-start | bytes 638984 | tf_op jit(solution)/shard_map/ppermute | solution.py:234
  69.2 4.2 %collective-permute-done.16 = bf16[208,512]{1,0:T(8,128)(2,1)S(1)} collective-permute-done((bf16[208,512]{1,0:T(8,128)(2,1)S(1)}, bf16[208,512]{1,0:T(8,128)(2,1)S(1)}, u32[]{:S(2)}, u32[]{:S(2)}) %collective-permute-start.16) | collective-permute-done | bytes 213024 | tf_op jit(solution)/shard_map/ppermute | solution.py:234
  73.7 0.7 convert_bitcast_fusion
  74.4 1.1 %fusion.4 = f32[512,512]{1,0:T(8,128)} fusion(bf16[416,512]{1,0:T(8,128)(2,1)S(1)} %maximum_select_fusion, bf16[416,512]{1,0:T(8,128)(2,1)S(1)} %collective-permute-done.10, pred[]{:T(512)S(6)} %eq.29), kind=kLoop, calls=%fused_computation.10 | loop fusion | flops 2621440 | bytes 1900545 | tf_op jit(solution)/shard_map/convert_element_type | solution.py:348
  76.2 1.1 %maximum_convert_fusion = f32[512,512]{1,0:T(8,128)} fusion(bf16[320,512]{1,0:T(8,128)(2,1)S(1)} %slice_select_fusion, bf16[192,512]{1,0:T(8,128)(2,1)S(1)} %slice_select_fusion.1), kind=kLoop, calls=%fused_computation.12 | loop fusion | flops 1048576 | bytes 1572864 | tf_op jit(solution)/shard_map/convert_element_type | solution.py:348
  77.3 1.1 %fusion.2 = f32[512,512]{1,0:T(8,128)} fusion(bf16[416,512]{1,0:T(8,128)(2,1)S(1)} %maximum_select_fusion.1, bf16[416,512]{1,0:T(8,128)(2,1)S(1)} %collective-permute-done.17, pred[]{:T(512)S(6)} %eq.29), kind=kLoop, calls=%fused_computation.6 | loop fusion | flops 2621440 | bytes 1900545 | tf_op jit(solution)/shard_map/convert_element_type | solution.py:348
  (60 shorter events, 6.6 us)
Async XLA Ops:
  0.6 6.2 %collective-permute-start = (bf16[256,512]{1,0:T(8,128)(2,1)}, bf16[256,512]{1,0:T(8,128)(2,1)S(1)}, u32[]{:S(2)}, u32[]{:S(2)}) collective-permute-start(bf16[256,512]{1,0:T(8,128)(2,1)} %own_h.1), channel_id=1, source_target_pairs={{0,1},{1,0},{2,3},{3,2},{4,5},{5,4},{6,7},{7,6},{8,9},{9,8},{10,11... | collective-permute-start | bytes 786440 | tf_op jit(solution)/shard_map/ppermute | solution.py:234
  1.2 10.0 %collective-permute-start.1 = (bf16[256,512]{1,0:T(8,128)(2,1)}, bf16[256,512]{1,0:T(8,128)(2,1)S(1)}, u32[]{:S(2)}, u32[]{:S(2)}) collective-permute-start(bf16[256,512]{1,0:T(8,128)(2,1)} %own_h.1), channel_id=1, source_target_pairs={{0,15},{1,2},{2,1},{3,4},{4,3},{5,6},{6,5},{7,8},{8,7},{9,10},{10,... | collective-permute-start | bytes 786440 | tf_op jit(solution)/shard_map/ppermute | solution.py:234
  29.3 2.0 %collective-permute-start.2 = (bf16[416,512]{1,0:T(8,128)(2,1)}, bf16[416,512]{1,0:T(8,128)(2,1)S(1)}, u32[]{:S(2)}, u32[]{:S(2)}) collective-permute-start(bf16[416,512]{1,0:T(8,128)(2,1)} %get-tuple-element.17), channel_id=1, source_target_pairs={{0,1},{1,0},{2,3},{3,2},{4,5},{5,4},{6,7},{7,6},{8,9},{9,8},{10,11... | collective-permute-start | bytes 1277960 | tf_op jit(solution)/shard_map/ppermute | solution.py:234
  29.4 4.9 %collective-permute-start.11 = (bf16[416,512]{1,0:T(8,128)(2,1)}, bf16[416,512]{1,0:T(8,128)(2,1)S(1)}, u32[]{:S(2)}, u32[]{:S(2)}) collective-permute-start(bf16[416,512]{1,0:T(8,128)(2,1)} %get-tuple-element.22), channel_id=1, source_target_pairs={{0,1},{1,0},{2,3},{3,2},{4,5},{5,4},{6,7},{7,6},{8,9},{9,8},{10,11... | collective-permute-start | bytes 1277960 | tf_op jit(solution)/shard_map/ppermute | solution.py:234
  29.9 32.9 %collective-permute-start.5 = (bf16[256,512]{1,0:T(8,128)(2,1)}, bf16[256,512]{1,0:T(8,128)(2,1)S(1)}, u32[]{:S(2)}, u32[]{:S(2)}) collective-permute-start(bf16[256,512]{1,0:T(8,128)(2,1)} %get-tuple-element.19), channel_id=1, source_target_pairs={{0,1},{1,0},{2,3},{3,2},{4,5},{5,4},{6,7},{7,6},{8,9},{9,8},{10,11... | collective-permute-start | bytes 786440 | tf_op jit(solution)/shard_map/ppermute | solution.py:234
  32.6 14.7 %copy-start.1 = (bf16[512,512]{1,0:T(8,128)(2,1)S(1)}, bf16[512,512]{1,0:T(8,128)(2,1)}, u32[]{:S(2)}) copy-start(bf16[512,512]{1,0:T(8,128)(2,1)} %w_dst_h.1) | copy-start | bytes 1572868
  32.7 14.7 %copy-start.7 = (bf16[1024,512]{1,0:T(8,128)(2,1)S(1)}, bf16[1024,512]{1,0:T(8,128)(2,1)}, u32[]{:S(2)}) copy-start(bf16[1024,512]{1,0:T(8,128)(2,1)} %get-tuple-element.15) | copy-start | bytes 3145732
  32.7 5.9 %collective-permute-start.3 = (bf16[208,512]{1,0:T(8,128)(2,1)S(1)}, bf16[208,512]{1,0:T(8,128)(2,1)S(1)}, u32[]{:S(2)}, u32[]{:S(2)}) collective-permute-start(bf16[208,512]{1,0:T(8,128)(2,1)S(1)} %dynamic-slice_convert_fusion.1), channel_id=1, source_target_pairs={{0,2},{1,5},{2,0},{3,7},{4,6},{5,1},{6,4},{7,3},{8,10},{9,13},{10,... | collective-permute-start | bytes 638984 | tf_op jit(solution)/shard_map/ppermute | solution.py:234
  35.4 6.4 %collective-permute-start.12 = (bf16[208,512]{1,0:T(8,128)(2,1)S(1)}, bf16[208,512]{1,0:T(8,128)(2,1)S(1)}, u32[]{:S(2)}, u32[]{:S(2)}) collective-permute-start(bf16[208,512]{1,0:T(8,128)(2,1)S(1)} %dynamic-slice_convert_fusion), channel_id=1, source_target_pairs={{0,2},{1,5},{2,0},{3,7},{4,6},{5,1},{6,4},{7,3},{8,10},{9,13},{10,... | collective-permute-start | bytes 638984 | tf_op jit(solution)/shard_map/ppermute | solution.py:234
  38.7 4.8 %collective-permute-start.4 = (bf16[104,512]{1,0:T(8,128)(2,1)S(1)}, bf16[104,512]{1,0:T(8,128)(2,1)S(1)}, u32[]{:S(2)}, u32[]{:S(2)}) collective-permute-start(bf16[104,512]{1,0:T(8,128)(2,1)S(1)} %dynamic-slice_convert_fusion.3), channel_id=1, source_target_pairs={{0,4},{1,3},{2,6},{3,1},{4,0},{5,7},{6,2},{7,5},{8,12},{9,11},{10,... | collective-permute-start | bytes 319496 | tf_op jit(solution)/shard_map/ppermute | solution.py:234
  41.9 20.8 %copy-start = (bf16[512,512]{1,0:T(8,128)(2,1)S(1)}, bf16[512,512]{1,0:T(8,128)(2,1)}, u32[]{:S(2)}) copy-start(bf16[512,512]{1,0:T(8,128)(2,1)} %w_src_h.1) | copy-start | bytes 1572868
  42.0 20.8 %copy-start.3 = (bf16[256,512]{1,0:T(8,128)(2,1)S(1)}, bf16[256,512]{1,0:T(8,128)(2,1)}, u32[]{:S(2)}) copy-start(bf16[256,512]{1,0:T(8,128)(2,1)} %get-tuple-element.18) | copy-start | bytes 786436
  42.0 7.5 %collective-permute-start.13 = (bf16[104,512]{1,0:T(8,128)(2,1)S(1)}, bf16[104,512]{1,0:T(8,128)(2,1)S(1)}, u32[]{:S(2)}, u32[]{:S(2)}) collective-permute-start(bf16[104,512]{1,0:T(8,128)(2,1)S(1)} %dynamic-slice_convert_fusion.2), channel_id=1, source_target_pairs={{0,4},{1,3},{2,6},{3,1},{4,0},{5,7},{6,2},{7,5},{8,12},{9,11},{10,... | collective-permute-start | bytes 319496 | tf_op jit(solution)/shard_map/ppermute | solution.py:234
  44.0 7.5 %collective-permute-start.7 = (bf16[104,512]{1,0:T(8,128)(2,1)S(1)}, bf16[104,512]{1,0:T(8,128)(2,1)S(1)}, u32[]{:S(2)}, u32[]{:S(2)}) collective-permute-start(bf16[104,512]{1,0:T(8,128)(2,1)S(1)} %add_convert_fusion.5), channel_id=1, source_target_pairs={{0,8},{1,9},{2,10},{3,11},{4,12},{5,13},{6,14},{7,15},{8,0},{9,1},... | collective-permute-start | bytes 319496 | tf_op jit(solution)/shard_map/ppermute | solution.py:234
  48.1 26.3 %copy-start.8 = (bf16[1024,512]{1,0:T(8,128)(2,1)}, bf16[1024,512]{1,0:T(8,128)(2,1)S(1)}, u32[]{:S(2)}) copy-start(bf16[1024,512]{1,0:T(8,128)(2,1)S(1)} %convolution_convert_fusion) | copy-start | bytes 3145732
  49.4 13.4 %collective-permute-start.6 = (bf16[256,512]{1,0:T(8,128)(2,1)S(1)}, bf16[256,512]{1,0:T(8,128)(2,1)S(1)}, u32[]{:S(2)}, u32[]{:S(2)}) collective-permute-start(bf16[256,512]{1,0:T(8,128)(2,1)S(1)} %broadcast_add_fusion), channel_id=1, source_target_pairs={{0,15},{1,2},{2,1},{3,4},{4,3},{5,6},{6,5},{7,8},{8,7},{9,10},{10,... | collective-permute-start | bytes 786440 | tf_op jit(solution)/shard_map/ppermute | solution.py:234
  49.5 10.4 %collective-permute-start.14 = (bf16[104,512]{1,0:T(8,128)(2,1)S(1)}, bf16[104,512]{1,0:T(8,128)(2,1)S(1)}, u32[]{:S(2)}, u32[]{:S(2)}) collective-permute-start(bf16[104,512]{1,0:T(8,128)(2,1)S(1)} %add_convert_fusion.3), channel_id=1, source_target_pairs={{0,8},{1,9},{2,10},{3,11},{4,12},{5,13},{6,14},{7,15},{8,0},{9,1},... | collective-permute-start | bytes 319496 | tf_op jit(solution)/shard_map/ppermute | solution.py:234
  51.5 8.5 %collective-permute-start.8 = (bf16[104,512]{1,0:T(8,128)(2,1)S(1)}, bf16[104,512]{1,0:T(8,128)(2,1)S(1)}, u32[]{:S(2)}, u32[]{:S(2)}) collective-permute-start(bf16[104,512]{1,0:T(8,128)(2,1)S(1)} %add_convert_fusion.4), channel_id=1, source_target_pairs={{0,4},{1,3},{2,6},{3,1},{4,0},{5,7},{6,2},{7,5},{8,12},{9,11},{10,... | collective-permute-start | bytes 319496 | tf_op jit(solution)/shard_map/ppermute | solution.py:234
  60.0 7.6 %collective-permute-start.15 = (bf16[104,512]{1,0:T(8,128)(2,1)S(1)}, bf16[104,512]{1,0:T(8,128)(2,1)S(1)}, u32[]{:S(2)}, u32[]{:S(2)}) collective-permute-start(bf16[104,512]{1,0:T(8,128)(2,1)S(1)} %fusion.8), channel_id=1, source_target_pairs={{0,4},{1,3},{2,6},{3,1},{4,0},{5,7},{6,2},{7,5},{8,12},{9,11},{10,... | collective-permute-start | bytes 319496 | tf_op jit(solution)/shard_map/ppermute | solution.py:234
  60.1 6.9 %collective-permute-start.9 = (bf16[208,512]{1,0:T(8,128)(2,1)S(1)}, bf16[208,512]{1,0:T(8,128)(2,1)S(1)}, u32[]{:S(2)}, u32[]{:S(2)}) collective-permute-start(bf16[208,512]{1,0:T(8,128)(2,1)S(1)} %maximum_select_fusion.2), channel_id=1, source_target_pairs={{0,2},{1,5},{2,0},{3,7},{4,6},{5,1},{6,4},{7,3},{8,10},{9,13},{10,... | collective-permute-start | bytes 638984 | tf_op jit(solution)/shard_map/ppermute | solution.py:234
  63.1 14.2 %copy-start.2 = (f32[256,512]{1,0:T(8,128)}, f32[256,512]{1,0:T(8,128)S(1)}, u32[]{:S(2)}) copy-start(f32[256,512]{1,0:T(8,128)S(1)} %fusion.6) | copy-start | bytes 1572868
  67.2 6.5 %collective-permute-start.10 = (bf16[416,512]{1,0:T(8,128)(2,1)S(1)}, bf16[416,512]{1,0:T(8,128)(2,1)S(1)}, u32[]{:S(2)}, u32[]{:S(2)}) collective-permute-start(bf16[416,512]{1,0:T(8,128)(2,1)S(1)} %maximum_select_fusion), channel_id=1, source_target_pairs={{0,1},{1,0},{2,3},{3,2},{4,5},{5,4},{6,7},{7,6},{8,9},{9,8},{10,11... | collective-permute-start | bytes 1277960 | tf_op jit(solution)/shard_map/ppermute | solution.py:234
  67.6 5.9 %collective-permute-start.16 = (bf16[208,512]{1,0:T(8,128)(2,1)S(1)}, bf16[208,512]{1,0:T(8,128)(2,1)S(1)}, u32[]{:S(2)}, u32[]{:S(2)}) collective-permute-start(bf16[208,512]{1,0:T(8,128)(2,1)S(1)} %fusion.7), channel_id=1, source_target_pairs={{0,2},{1,5},{2,0},{3,7},{4,6},{5,1},{6,4},{7,3},{8,10},{9,13},{10,... | collective-permute-start | bytes 638984 | tf_op jit(solution)/shard_map/ppermute | solution.py:234
  73.6 2.5 %collective-permute-start.17 = (bf16[416,512]{1,0:T(8,128)(2,1)S(1)}, bf16[416,512]{1,0:T(8,128)(2,1)S(1)}, u32[]{:S(2)}, u32[]{:S(2)}) collective-permute-start(bf16[416,512]{1,0:T(8,128)(2,1)S(1)} %maximum_select_fusion.1), channel_id=1, source_target_pairs={{0,1},{1,0},{2,3},{3,2},{4,5},{5,4},{6,7},{7,6},{8,9},{9,8},{10,11... | collective-permute-start | bytes 1277960 | tf_op jit(solution)/shard_map/ppermute | solution.py:234
  (3 other events, 14.4 us)

commit v4 on v3

--- a/solution.py
+++ b/solution.py
@@ -49,8 +49,8 @@
 
 def edge_kernel(
     tiles, edge_h, grid_h, cot_h, src_h, own_h, chip_h, next_h, w_src_h, w_edge_h, w_dst_h, w_out_h, bias_h,
-    send_a, keep_a, send_b, keep_b, own_sum_h, to_chip_h, to_next_h, d_node_h,
-    edge, grid, cot, src, near_rows, w_src, w_dst, w_out, bias, rhs, wide, pre, node_term, d_pre, d_node, packed, sums, *rest,
+    send_a, keep_a, send_b, keep_b, own_sum, to_chip, to_next, d_node,
+    edge, grid, cot, src, near_rows, w_src, w_dst, w_out, bias, rhs, wide, pre, node_term, d_pre, packed, sums, *rest,
 ):
     lhs, pick_t = rest[:tiles], rest[tiles : 2 * tiles]
     acc, g_edge, g_dst, g_out, g_bias, sems, near_sems, in_sems, out_sems = rest[2 * tiles :]
@@ -174,8 +174,7 @@
         kept = pl.ds(pl.multiple_of(start + odd * half, 8), half)
         pairs += [(packed.at[gone, :], send), (packed.at[kept, :], keep)]
         start += 2 * half
-    pairs += [(sums.at[1], own_sum_h), (sums.at[2 - 2 * odd], to_chip_h)]
-    pairs += [(sums.at[2 * odd], to_next_h), (d_node, d_node_h)]
+    pairs += [(sums.at[1], own_sum), (sums.at[2 - 2 * odd], to_chip), (sums.at[2 * odd], to_next)]
     for copy in copies(out_sems, pairs):
         copy.wait()
 
@@ -191,8 +190,8 @@
     return pl.pallas_call(
         functools.partial(edge_kernel, tiles),
         in_specs=[HBM] * 12,
-        out_specs=[HBM] * len(shapes),
-        out_shape=[jax.ShapeDtypeStruct(shape, BF16) for shape in shapes],
+        out_specs=[VMEM] * len(shapes),
+        out_shape=[pltpu.VMEM(shape, BF16) for shape in shapes],
         scratch_shapes=[
             pltpu.VMEM(edge.shape, BF16),
             pltpu.VMEM((nodes, width), BF16),
@@ -208,7 +207,6 @@
             pltpu.VMEM((fan, nodes, width), F32),
             pltpu.VMEM((nodes, width), F32),
             pltpu.VMEM((fan, nodes, width), BF16),
-            pltpu.VMEM((nodes, width), BF16),
             pltpu.VMEM((sum(chain_rows), width), BF16),
             pltpu.VMEM((3, owned, width), BF16),
         ]
@@ -223,7 +221,7 @@
             pltpu.SemaphoreType.DMA((2, 5)),
             pltpu.SemaphoreType.DMA((3,)),
             pltpu.SemaphoreType.DMA((tiles, 2)),
-            pltpu.SemaphoreType.DMA((8,)),
+            pltpu.SemaphoreType.DMA((7,)),
         ],
         compiler_params=params(),
         name="edge_terms",
@@ -256,8 +254,8 @@
 
 
 def after(value, other):
-    corner = other[(slice(0, 1),) * other.ndim].reshape((1,) * value.ndim)
-    return value + jnp.minimum(jnp.abs(corner), 0).astype(value.dtype)
+    nothing = jnp.minimum(jnp.abs(other[:16]), 0).astype(value.dtype)
+    return value + jnp.pad(nothing, ((0, value.shape[0] - nothing.shape[0]), (0, 0)))
 
 
 class Chain:
@@ -322,21 +320,22 @@
     for level in range(1, len(stages) - 1):
         a.halve()
         b.halve()
+    from_next = exchanged(after(to_next, a.block), beyond)
     a.swap()
     b.swap()
-    from_next = exchanged(after(to_next, a.block), beyond)
     from_chip = exchanged(to_chip, chip)
     d_mesh_in = sum(x.astype(F32) for x in (own_sum, from_chip, from_next))
     d_mesh = dot(d_mesh_in.astype(BF16), w_src, NT)
     d_grid = dot(after(d_node, a.block), w_dst, NT).astype(BF16)
-    a.double()
-    b.double(d_grid)
+    for level in range(1, len(stages) - 1):
+        a.double(b.block)
+    b.double(a.block, d_grid)
     for level in range(2, len(stages) - 1):
-        a.double()
-        b.double(d_mesh)
-    a.double()
-    b.double()
+        b.double()
     starts = [sum(chain_rows) - i * width for i in (3, 2, 1, 0)]
+    a.double(b.block, d_mesh)
+    d_w_src = a.joined(starts[0], starts[1]).astype(F32)
+    b.double(d_w_src)
 
     def rows_of(start, stop):
         cut = chain_rows[0]
@@ -350,7 +349,7 @@
     return (
         d_grid,
         d_mesh,
-        rows_of(starts[0], starts[1]),
+        d_w_src,
         rows_of(starts[1], starts[2]),
         rows_of(starts[2], starts[3]),
         rows_of(outs, outs + 1)[0],

time: 78.7 us -> 74.9 us (0.952)
  starting transfers between devices: 21.6 us -> 25.3 us
  waiting for transfers between devices: 25.1 us -> 22.8 us
  between operations: 2.96 us -> 0.93 us
  other arithmetic: 7.72 us -> 6 us
  local copies, waits for them, and re-layouts: 2.51 us -> 0.86 us
    ppermute x18, starting transfers between devices: 21.6 us -> 25.3 us  [exchanged(): return lax.ppermute(block, 'region', pairs)]
    ppermute x18, waiting for transfers between devices: 25.1 us -> 22.8 us  [exchanged(): return lax.ppermute(block, 'region', pairs)]
    convert_element_type x3 -> x1, other arithmetic: 3.33 us -> 1.61 us  [rows_of(): return jnp.concatenate(parts).astype(F32)]
    slice x3 -> x0, local copies, waits for them, and re-layouts: 1.65 us -> none  [after(): corner = other[(slice(0, 1),) * other.ndim].reshape((1,) * value.ndim)]
  transfers between devices with their start and end apart: 18 -> 18, of which waited for: 8 -> 10; matrix products, arithmetic and copies ran while one was open for 11% -> 7% of each run, Pallas kernels for 0% -> 0%
where the time goes in v4:
time: 74.9 us; the launch traced here: 74.6 us
  starting transfers between devices  25.3 us (34%)
  waiting for transfers between devices  22.8 us (30%)
  Pallas kernels  17.6 us (23%)
  other arithmetic  6 us (8%)
  matrix products  1.09 us (1%)
  between operations  0.93 us (1%)
  local copies, waits for them, and re-layouts  0.86 us (1%)
    ppermute x18, starting transfers between devices, exchanged(): return lax.ppermute(block, 'region', pairs)  25.3 us
    ppermute x18, waiting for transfers between devices, exchanged(): return lax.ppermute(block, 'region', pairs)  22.8 us
    pallas_call x1, Pallas kernels, edge_call(): pl.pallas_call(functools.partial(edge_kernel, tiles), in_specs=[HBM] * 12...  17.6 us
    add x4, other arithmetic, total(): return self.block.astype(F32) + self.arrived.astype(F32)  2.35 us
    convert_element_type x1, other arithmetic, rows_of(): return jnp.concatenate(parts).astype(F32)  1.61 us
  transfers between devices with their start and end apart: 18, of which 10 were waited for; matrix products, arithmetic and copies ran while one was open for 7% of the time, Pallas kernels for 0%

profile of v4, /device:TPU:0, one launch (start us, length us, event | category | flops | bytes accessed | tf_op | source)
XLA Modules:
  0.0 74.6 jit_solution(13063109668556957393)
XLA Ops:
  1.2 5.7 %collective-permute-start.1 = (bf16[256,512]{1,0:T(8,128)(2,1)}, bf16[256,512]{1,0:T(8,128)(2,1)S(1)}, u32[]{:S(2)}, u32[]{:S(2)}) collective-permute-start(bf16[256,512]{1,0:T(8,128)(2,1)} %own_h.1), channel_id=1, source_target_pairs={{0,15},{1,2},{2,1},{3,4},{4,3},{5,6},{6,5},{7,8},{8,7},{9,10},{10,... | collective-permute-start | bytes 786440 | tf_op jit(solution)/shard_map/ppermute | solution.py:232
  6.8 4.3 %collective-permute-done.1.next_h = bf16[256,512]{1,0:T(8,128)(2,1)S(1)} collective-permute-done((bf16[256,512]{1,0:T(8,128)(2,1)}, bf16[256,512]{1,0:T(8,128)(2,1)S(1)}, u32[]{:S(2)}, u32[]{:S(2)}) %collective-permute-start.1) | collective-permute-done | bytes 262176 | tf_op jit(solution)/shard_map/ppermute | solution.py:232
  11.1 0.7 copy-done.5
  11.8 17.6 %edge_terms.1 = (bf16[416,512]{1,0:T(8,128)(2,1)}, bf16[416,512]{1,0:T(8,128)(2,1)S(1)}, bf16[416,512]{1,0:T(8,128)(2,1)S(1)}, bf16[416,512]{1,0:T(8,128)(2,1)S(...) custom-call(bf16[3072,512]{1,0:T(8,128)(2,1)} %edge_h.1, ...), custom_call_target="tpu_custom_call" | custom-call | tf_op jit(solution)/shard_map/edge_terms/pallas_call | solution.py:190
  30.1 1.5 %collective-permute-done.2 = bf16[416,512]{1,0:T(8,128)(2,1)} collective-permute-done((bf16[416,512]{1,0:T(8,128)(2,1)}, bf16[416,512]{1,0:T(8,128)(2,1)}, u32[]{:S(2)}, u32[]{:S(2)}) %collective-permute-start.2) | collective-permute-done | bytes 426016 | tf_op jit(solution)/shard_map/ppermute | solution.py:232
  31.6 1.1 %convert_add_fusion.1 = f32[416,512]{1,0:T(8,128)S(1)} fusion(bf16[416,512]{1,0:T(8,128)(2,1)} %collective-permute-done.2, bf16[416,512]{1,0:T(8,128)(2,1)S(1)} %get-tuple-element.16), kind=kLoop, calls=%fused_computation.4 | loop fusion | flops 638976 | bytes 1703936 | tf_op jit(solution)/shard_map/add | solution.py:267
  32.8 1.5 %collective-permute-start.3 = (bf16[208,512]{1,0:T(8,128)(2,1)S(1)}, bf16[208,512]{1,0:T(8,128)(2,1)S(1)}, u32[]{:S(2)}, u32[]{:S(2)}) collective-permute-start(bf16[208,512]{1,0:T(8,128)(2,1)S(1)} %dynamic-slice_convert_fusion.1), channel_id=1, source_target_pairs={{0,2},{1,5},{2,0},{3,7},{4,6},{5,1},{6,4},{7,3},{8,10},{9,13},{10,... | collective-permute-start | bytes 638984 | tf_op jit(solution)/shard_map/ppermute | solution.py:232
  34.3 1.1 %convert_add_fusion = f32[416,512]{1,0:T(8,128)S(1)} fusion(bf16[416,512]{1,0:T(8,128)(2,1)} %collective-permute-done.8, bf16[416,512]{1,0:T(8,128)(2,1)S(1)} %get-tuple-element.21), kind=kLoop, calls=%fused_computation.3 | loop fusion | flops 638976 | bytes 1703936 | tf_op jit(solution)/shard_map/add | solution.py:267
  36.1 2.6 %collective-permute-done.3 = bf16[208,512]{1,0:T(8,128)(2,1)S(1)} collective-permute-done((bf16[208,512]{1,0:T(8,128)(2,1)S(1)}, bf16[208,512]{1,0:T(8,128)(2,1)S(1)}, u32[]{:S(2)}, u32[]{:S(2)}) %collective-permute-start.3) | collective-permute-done | bytes 213024 | tf_op jit(solution)/shard_map/ppermute | solution.py:232
  38.8 1.7 %collective-permute-start.4 = (bf16[104,512]{1,0:T(8,128)(2,1)S(1)}, bf16[104,512]{1,0:T(8,128)(2,1)S(1)}, u32[]{:S(2)}, u32[]{:S(2)}) collective-permute-start(bf16[104,512]{1,0:T(8,128)(2,1)S(1)} %dynamic-slice_convert_fusion.3), channel_id=1, source_target_pairs={{0,4},{1,3},{2,6},{3,1},{4,0},{5,7},{6,2},{7,5},{8,12},{9,11},{10,... | collective-permute-start | bytes 319496 | tf_op jit(solution)/shard_map/ppermute | solution.py:232
  40.5 2.4 %collective-permute-start.6 = (bf16[256,512]{1,0:T(8,128)(2,1)S(1)}, bf16[256,512]{1,0:T(8,128)(2,1)S(1)}, u32[]{:S(2)}, u32[]{:S(2)}) collective-permute-start(bf16[256,512]{1,0:T(8,128)(2,1)S(1)} %pad_add_fusion), channel_id=1, source_target_pairs={{0,15},{1,2},{2,1},{3,4},{4,3},{5,6},{6,5},{7,8},{8,7},{9,10},{10,... | collective-permute-start | bytes 786440 | tf_op jit(solution)/shard_map/ppermute | solution.py:232
  43.6 2.6 %collective-permute-start.7 = (bf16[104,512]{1,0:T(8,128)(2,1)S(1)}, bf16[104,512]{1,0:T(8,128)(2,1)S(1)}, u32[]{:S(2)}, u32[]{:S(2)}) collective-permute-start(bf16[104,512]{1,0:T(8,128)(2,1)S(1)} %add_convert_fusion.5), channel_id=1, source_target_pairs={{0,8},{1,9},{2,10},{3,11},{4,12},{5,13},{6,14},{7,15},{8,0},{9,1},... | collective-permute-start | bytes 319496 | tf_op jit(solution)/shard_map/ppermute | solution.py:232
  46.3 2.8 %collective-permute-done.10 = bf16[104,512]{1,0:T(8,128)(2,1)S(1)} collective-permute-done((bf16[104,512]{1,0:T(8,128)(2,1)S(1)}, bf16[104,512]{1,0:T(8,128)(2,1)S(1)}, u32[]{:S(2)}, u32[]{:S(2)}) %collective-permute-start.10) | collective-permute-done | bytes 106528 | tf_op jit(solution)/shard_map/ppermute | solution.py:232
  49.1 2.3 %collective-permute-start.13 = (bf16[104,512]{1,0:T(8,128)(2,1)S(1)}, bf16[104,512]{1,0:T(8,128)(2,1)S(1)}, u32[]{:S(2)}, u32[]{:S(2)}) collective-permute-start(bf16[104,512]{1,0:T(8,128)(2,1)S(1)} %add_convert_fusion.3), channel_id=1, source_target_pairs={{0,8},{1,9},{2,10},{3,11},{4,12},{5,13},{6,14},{7,15},{8,0},{9,1},... | collective-permute-start | bytes 319496 | tf_op jit(solution)/shard_map/ppermute | solution.py:232
  51.4 0.7 convolution_convert_fusion
  52.2 1.5 %collective-permute-start.11 = (bf16[104,512]{1,0:T(8,128)(2,1)S(1)}, bf16[104,512]{1,0:T(8,128)(2,1)S(1)}, u32[]{:S(2)}, u32[]{:S(2)}) collective-permute-start(bf16[104,512]{1,0:T(8,128)(2,1)S(1)} %fusion.11), channel_id=1, source_target_pairs={{0,4},{1,3},{2,6},{3,1},{4,0},{5,7},{6,2},{7,5},{8,12},{9,11},{10,... | collective-permute-start | bytes 319496 | tf_op jit(solution)/shard_map/ppermute | solution.py:232
  54.2 3.6 %collective-permute-done.11 = bf16[104,512]{1,0:T(8,128)(2,1)S(1)} collective-permute-done((bf16[104,512]{1,0:T(8,128)(2,1)S(1)}, bf16[104,512]{1,0:T(8,128)(2,1)S(1)}, u32[]{:S(2)}, u32[]{:S(2)}) %collective-permute-start.11) | collective-permute-done | bytes 106528 | tf_op jit(solution)/shard_map/ppermute | solution.py:232
  57.9 0.8 %collective-permute-start.14 = (bf16[104,512]{1,0:T(8,128)(2,1)S(1)}, bf16[104,512]{1,0:T(8,128)(2,1)S(1)}, u32[]{:S(2)}, u32[]{:S(2)}) collective-permute-start(bf16[104,512]{1,0:T(8,128)(2,1)S(1)} %fusion.13), channel_id=1, source_target_pairs={{0,4},{1,3},{2,6},{3,1},{4,0},{5,7},{6,2},{7,5},{8,12},{9,11},{10,... | collective-permute-start | bytes 319496 | tf_op jit(solution)/shard_map/ppermute | solution.py:232
  58.7 2.3 %collective-permute-start.12 = (bf16[208,512]{1,0:T(8,128)(2,1)S(1)}, bf16[208,512]{1,0:T(8,128)(2,1)S(1)}, u32[]{:S(2)}, u32[]{:S(2)}) collective-permute-start(bf16[208,512]{1,0:T(8,128)(2,1)S(1)} %fusion.10), channel_id=1, source_target_pairs={{0,2},{1,5},{2,0},{3,7},{4,6},{5,1},{6,4},{7,3},{8,10},{9,13},{10,... | collective-permute-start | bytes 638984 | tf_op jit(solution)/shard_map/ppermute | solution.py:232
  61.0 2.3 %collective-permute-done.14 = bf16[104,512]{1,0:T(8,128)(2,1)S(1)} collective-permute-done((bf16[104,512]{1,0:T(8,128)(2,1)S(1)}, bf16[104,512]{1,0:T(8,128)(2,1)S(1)}, u32[]{:S(2)}, u32[]{:S(2)}) %collective-permute-start.14) | collective-permute-done | bytes 106528 | tf_op jit(solution)/shard_map/ppermute | solution.py:232
  63.4 1.4 %collective-permute-done.12 = bf16[208,512]{1,0:T(8,128)(2,1)S(1)} collective-permute-done((bf16[208,512]{1,0:T(8,128)(2,1)S(1)}, bf16[208,512]{1,0:T(8,128)(2,1)S(1)}, u32[]{:S(2)}, u32[]{:S(2)}) %collective-permute-start.12) | collective-permute-done | bytes 213024 | tf_op jit(solution)/shard_map/ppermute | solution.py:232
  65.1 2.0 %collective-permute-start.16 = (bf16[208,512]{1,0:T(8,128)(2,1)S(1)}, bf16[208,512]{1,0:T(8,128)(2,1)S(1)}, u32[]{:S(2)}, u32[]{:S(2)}) collective-permute-start(bf16[208,512]{1,0:T(8,128)(2,1)S(1)} %maximum_select_fusion.3), channel_id=1, source_target_pairs={{0,2},{1,5},{2,0},{3,7},{4,6},{5,1},{6,4},{7,3},{8,10},{9,13},{10,... | collective-permute-start | bytes 638984 | tf_op jit(solution)/shard_map/ppermute | solution.py:232
  67.3 3.7 %collective-permute-done.16 = bf16[208,512]{1,0:T(8,128)(2,1)S(1)} collective-permute-done((bf16[208,512]{1,0:T(8,128)(2,1)S(1)}, bf16[208,512]{1,0:T(8,128)(2,1)S(1)}, u32[]{:S(2)}, u32[]{:S(2)}) %collective-permute-start.16) | collective-permute-done | bytes 213024 | tf_op jit(solution)/shard_map/ppermute | solution.py:232
  73.0 1.6 %fusion.3 = (f32[512,512]{1,0:T(8,128)}, f32[512,512]{1,0:T(8,128)}) fusion(bf16[416,512]{1,0:T(8,128)(2,1)S(1)} %fusion.8, bf16[416,512]{1,0:T(8,128)(2,1)S(1)} %collective-permute-done.17, pred[]{:T(512)S(6)} %eq.29, bf16[320,512]{1,0:T(8,128)(2,1)S(1)} %slice_select_fusion, bf16[192,512]{1,0:T(8,128)(2,1)S(1)} %slice_select_fusion.1), kind=kLoop, calls=%fused_computation.7 | loop fusion | flops 3670016 | bytes 3473409 | tf_op jit(solution)/shard_map/convert_element_type | solution.py:347
  (60 shorter events, 5.8 us)
Async XLA Ops:
  0.6 6.2 %collective-permute-start = (bf16[256,512]{1,0:T(8,128)(2,1)}, bf16[256,512]{1,0:T(8,128)(2,1)S(1)}, u32[]{:S(2)}, u32[]{:S(2)}) collective-permute-start(bf16[256,512]{1,0:T(8,128)(2,1)} %own_h.1), channel_id=1, source_target_pairs={{0,1},{1,0},{2,3},{3,2},{4,5},{5,4},{6,7},{7,6},{8,9},{9,8},{10,11... | collective-permute-start | bytes 786440 | tf_op jit(solution)/shard_map/ppermute | solution.py:232
  1.2 10.0 %collective-permute-start.1 = (bf16[256,512]{1,0:T(8,128)(2,1)}, bf16[256,512]{1,0:T(8,128)(2,1)S(1)}, u32[]{:S(2)}, u32[]{:S(2)}) collective-permute-start(bf16[256,512]{1,0:T(8,128)(2,1)} %own_h.1), channel_id=1, source_target_pairs={{0,15},{1,2},{2,1},{3,4},{4,3},{5,6},{6,5},{7,8},{8,7},{9,10},{10,... | collective-permute-start | bytes 786440 | tf_op jit(solution)/shard_map/ppermute | solution.py:232
  6.8 5.0 %copy-start.4 = (bf16[256,512]{1,0:T(8,128)(2,1)}, bf16[256,512]{1,0:T(8,128)(2,1)S(1)}, u32[]{:S(2)}) copy-start(bf16[256,512]{1,0:T(8,128)(2,1)S(1)} %collective-permute-done.chip_h) | copy-start | bytes 786436
  29.4 2.2 %collective-permute-start.2 = (bf16[416,512]{1,0:T(8,128)(2,1)}, bf16[416,512]{1,0:T(8,128)(2,1)}, u32[]{:S(2)}, u32[]{:S(2)}) collective-permute-start(bf16[416,512]{1,0:T(8,128)(2,1)} %get-tuple-element.17), channel_id=1, source_target_pairs={{0,1},{1,0},{2,3},{3,2},{4,5},{5,4},{6,7},{7,6},{8,9},{9,8},{10,11... | collective-permute-start | bytes 1277960 | tf_op jit(solution)/shard_map/ppermute | solution.py:232
  29.5 4.8 %collective-permute-start.8 = (bf16[416,512]{1,0:T(8,128)(2,1)S(1)}, bf16[416,512]{1,0:T(8,128)(2,1)}, u32[]{:S(2)}, u32[]{:S(2)}) collective-permute-start(bf16[416,512]{1,0:T(8,128)(2,1)S(1)} %get-tuple-element.22), channel_id=1, source_target_pairs={{0,1},{1,0},{2,3},{3,2},{4,5},{5,4},{6,7},{7,6},{8,9},{9,8},{10,11... | collective-permute-start | bytes 1277960 | tf_op jit(solution)/shard_map/ppermute | solution.py:232
  30.0 23.8 %collective-permute-start.5 = (bf16[256,512]{1,0:T(8,128)(2,1)S(1)}, bf16[256,512]{1,0:T(8,128)(2,1)S(1)}, u32[]{:S(2)}, u32[]{:S(2)}) collective-permute-start(bf16[256,512]{1,0:T(8,128)(2,1)S(1)} %get-tuple-element.19), channel_id=1, source_target_pairs={{0,1},{1,0},{2,3},{3,2},{4,5},{5,4},{6,7},{7,6},{8,9},{9,8},{10,11... | collective-permute-start | bytes 786440 | tf_op jit(solution)/shard_map/ppermute | solution.py:232
  32.8 5.9 %collective-permute-start.3 = (bf16[208,512]{1,0:T(8,128)(2,1)S(1)}, bf16[208,512]{1,0:T(8,128)(2,1)S(1)}, u32[]{:S(2)}, u32[]{:S(2)}) collective-permute-start(bf16[208,512]{1,0:T(8,128)(2,1)S(1)} %dynamic-slice_convert_fusion.1), channel_id=1, source_target_pairs={{0,2},{1,5},{2,0},{3,7},{4,6},{5,1},{6,4},{7,3},{8,10},{9,13},{10,... | collective-permute-start | bytes 638984 | tf_op jit(solution)/shard_map/ppermute | solution.py:232
  35.5 15.9 %copy-start.3 = (bf16[512,512]{1,0:T(8,128)(2,1)S(1)}, bf16[512,512]{1,0:T(8,128)(2,1)}, u32[]{:S(2)}) copy-start(bf16[512,512]{1,0:T(8,128)(2,1)} %w_dst_h.1) | copy-start | bytes 1572868
  35.5 7.4 %collective-permute-start.9 = (bf16[208,512]{1,0:T(8,128)(2,1)S(1)}, bf16[208,512]{1,0:T(8,128)(2,1)S(1)}, u32[]{:S(2)}, u32[]{:S(2)}) collective-permute-start(bf16[208,512]{1,0:T(8,128)(2,1)S(1)} %dynamic-slice_convert_fusion), channel_id=1, source_target_pairs={{0,2},{1,5},{2,0},{3,7},{4,6},{5,1},{6,4},{7,3},{8,10},{9,13},{10,... | collective-permute-start | bytes 638984 | tf_op jit(solution)/shard_map/ppermute | solution.py:232
  38.8 4.8 %collective-permute-start.4 = (bf16[104,512]{1,0:T(8,128)(2,1)S(1)}, bf16[104,512]{1,0:T(8,128)(2,1)S(1)}, u32[]{:S(2)}, u32[]{:S(2)}) collective-permute-start(bf16[104,512]{1,0:T(8,128)(2,1)S(1)} %dynamic-slice_convert_fusion.3), channel_id=1, source_target_pairs={{0,4},{1,3},{2,6},{3,1},{4,0},{5,7},{6,2},{7,5},{8,12},{9,11},{10,... | collective-permute-start | bytes 319496 | tf_op jit(solution)/shard_map/ppermute | solution.py:232
  40.5 13.3 %collective-permute-start.6 = (bf16[256,512]{1,0:T(8,128)(2,1)S(1)}, bf16[256,512]{1,0:T(8,128)(2,1)S(1)}, u32[]{:S(2)}, u32[]{:S(2)}) collective-permute-start(bf16[256,512]{1,0:T(8,128)(2,1)S(1)} %pad_add_fusion), channel_id=1, source_target_pairs={{0,15},{1,2},{2,1},{3,4},{4,3},{5,6},{6,5},{7,8},{8,7},{9,10},{10,... | collective-permute-start | bytes 786440 | tf_op jit(solution)/shard_map/ppermute | solution.py:232
  43.0 6.1 %collective-permute-start.10 = (bf16[104,512]{1,0:T(8,128)(2,1)S(1)}, bf16[104,512]{1,0:T(8,128)(2,1)S(1)}, u32[]{:S(2)}, u32[]{:S(2)}) collective-permute-start(bf16[104,512]{1,0:T(8,128)(2,1)S(1)} %dynamic-slice_convert_fusion.2), channel_id=1, source_target_pairs={{0,4},{1,3},{2,6},{3,1},{4,0},{5,7},{6,2},{7,5},{8,12},{9,11},{10,... | collective-permute-start | bytes 319496 | tf_op jit(solution)/shard_map/ppermute | solution.py:232
  43.6 8.6 %collective-permute-start.7 = (bf16[104,512]{1,0:T(8,128)(2,1)S(1)}, bf16[104,512]{1,0:T(8,128)(2,1)S(1)}, u32[]{:S(2)}, u32[]{:S(2)}) collective-permute-start(bf16[104,512]{1,0:T(8,128)(2,1)S(1)} %add_convert_fusion.5), channel_id=1, source_target_pairs={{0,8},{1,9},{2,10},{3,11},{4,12},{5,13},{6,14},{7,15},{8,0},{9,1},... | collective-permute-start | bytes 319496 | tf_op jit(solution)/shard_map/ppermute | solution.py:232
  49.1 8.7 %collective-permute-start.13 = (bf16[104,512]{1,0:T(8,128)(2,1)S(1)}, bf16[104,512]{1,0:T(8,128)(2,1)S(1)}, u32[]{:S(2)}, u32[]{:S(2)}) collective-permute-start(bf16[104,512]{1,0:T(8,128)(2,1)S(1)} %add_convert_fusion.3), channel_id=1, source_target_pairs={{0,8},{1,9},{2,10},{3,11},{4,12},{5,13},{6,14},{7,15},{8,0},{9,1},... | collective-permute-start | bytes 319496 | tf_op jit(solution)/shard_map/ppermute | solution.py:232
  51.4 2.4 %copy-start = (bf16[512,512]{1,0:T(8,128)(2,1)S(1)}, bf16[512,512]{1,0:T(8,128)(2,1)}, u32[]{:S(2)}) copy-start(bf16[512,512]{1,0:T(8,128)(2,1)} %w_src_h.1) | copy-start | bytes 1572868
  52.2 12.8 %copy-start.6 = (bf16[1024,512]{1,0:T(8,128)(2,1)}, bf16[1024,512]{1,0:T(8,128)(2,1)S(1)}, u32[]{:S(2)}) copy-start(bf16[1024,512]{1,0:T(8,128)(2,1)S(1)} %convolution_convert_fusion) | copy-start | bytes 3145732
  52.2 5.5 %collective-permute-start.11 = (bf16[104,512]{1,0:T(8,128)(2,1)S(1)}, bf16[104,512]{1,0:T(8,128)(2,1)S(1)}, u32[]{:S(2)}, u32[]{:S(2)}) collective-permute-start(bf16[104,512]{1,0:T(8,128)(2,1)S(1)} %fusion.11), channel_id=1, source_target_pairs={{0,4},{1,3},{2,6},{3,1},{4,0},{5,7},{6,2},{7,5},{8,12},{9,11},{10,... | collective-permute-start | bytes 319496 | tf_op jit(solution)/shard_map/ppermute | solution.py:232
  54.1 17.0 %copy-start.2 = (f32[256,512]{1,0:T(8,128)}, f32[256,512]{1,0:T(8,128)S(1)}, u32[]{:S(2)}) copy-start(f32[256,512]{1,0:T(8,128)S(1)} %fusion.9) | copy-start | bytes 1572868
  57.9 5.4 %collective-permute-start.14 = (bf16[104,512]{1,0:T(8,128)(2,1)S(1)}, bf16[104,512]{1,0:T(8,128)(2,1)S(1)}, u32[]{:S(2)}, u32[]{:S(2)}) collective-permute-start(bf16[104,512]{1,0:T(8,128)(2,1)S(1)} %fusion.13), channel_id=1, source_target_pairs={{0,4},{1,3},{2,6},{3,1},{4,0},{5,7},{6,2},{7,5},{8,12},{9,11},{10,... | collective-permute-start | bytes 319496 | tf_op jit(solution)/shard_map/ppermute | solution.py:232
  58.7 6.1 %collective-permute-start.12 = (bf16[208,512]{1,0:T(8,128)(2,1)S(1)}, bf16[208,512]{1,0:T(8,128)(2,1)S(1)}, u32[]{:S(2)}, u32[]{:S(2)}) collective-permute-start(bf16[208,512]{1,0:T(8,128)(2,1)S(1)} %fusion.10), channel_id=1, source_target_pairs={{0,2},{1,5},{2,0},{3,7},{4,6},{5,1},{6,4},{7,3},{8,10},{9,13},{10,... | collective-permute-start | bytes 638984 | tf_op jit(solution)/shard_map/ppermute | solution.py:232
  65.0 2.2 %collective-permute-start.15 = (bf16[416,512]{1,0:T(8,128)(2,1)S(1)}, bf16[416,512]{1,0:T(8,128)(2,1)S(1)}, u32[]{:S(2)}, u32[]{:S(2)}) collective-permute-start(bf16[416,512]{1,0:T(8,128)(2,1)S(1)} %fusion.7), channel_id=1, source_target_pairs={{0,1},{1,0},{2,3},{3,2},{4,5},{5,4},{6,7},{7,6},{8,9},{9,8},{10,11... | collective-permute-start | bytes 1277960 | tf_op jit(solution)/shard_map/ppermute | solution.py:232
  65.1 5.8 %collective-permute-start.16 = (bf16[208,512]{1,0:T(8,128)(2,1)S(1)}, bf16[208,512]{1,0:T(8,128)(2,1)S(1)}, u32[]{:S(2)}, u32[]{:S(2)}) collective-permute-start(bf16[208,512]{1,0:T(8,128)(2,1)S(1)} %maximum_select_fusion.3), channel_id=1, source_target_pairs={{0,2},{1,5},{2,0},{3,7},{4,6},{5,1},{6,4},{7,3},{8,10},{9,13},{10,... | collective-permute-start | bytes 638984 | tf_op jit(solution)/shard_map/ppermute | solution.py:232
  67.3 7.4 %copy-start.1 = (f32[512,512]{1,0:T(8,128)}, f32[512,512]{1,0:T(8,128)S(1)}, u32[]{:S(2)}) copy-start(f32[512,512]{1,0:T(8,128)S(1)} %fusion.5) | copy-start | bytes 3145732
  71.2 1.8 %collective-permute-start.17 = (bf16[416,512]{1,0:T(8,128)(2,1)S(1)}, bf16[416,512]{1,0:T(8,128)(2,1)S(1)}, u32[]{:S(2)}, u32[]{:S(2)}) collective-permute-start(bf16[416,512]{1,0:T(8,128)(2,1)S(1)} %fusion.8), channel_id=1, source_target_pairs={{0,1},{1,0},{2,3},{3,2},{4,5},{5,4},{6,7},{7,6},{8,9},{9,8},{10,11... | collective-permute-start | bytes 1277960 | tf_op jit(solution)/shard_map/ppermute | solution.py:232
  (1 other events, 0.7 us)
